TPU v7x, 32 devices: a whole 2x2x4 slice. The times are simulated.
32 devices in a mesh: grp: 2 (over core), row: 4 (over y, x), col: 4 (over z).
Axes of the slice: x: 2, y: 2, z: 4, core: 2. Of those that a mesh axis runs over, the one named last changes fastest.
Arguments:
- iterate: bfloat16 [8192, 7168], P(('grp', 'row'), 'col'), parts along dimension 0, may hold values from -0.046875 to 0.046875
Outputs:
- update: bfloat16 [8192, 7168], P(('grp', 'row'), 'col'), parts along dimension 0
There are 2 independent parts, one for each index of `grp`. A program takes and returns all parts, laid end to end along the dimension named above; each array names one. Nothing has to cross between parts.
All inputs are finite; a program needn't handle non-finite values.
Results may differ from a plain program's by a relative error of at most 0.0076.
Values may be sent and summed in bfloat16 or wider, within the bound.
A program may use at most 128 MiB of HBM per device.

v0:
```python
import math

import jax
import jax.numpy as jnp
from jax import lax
from jax.sharding import PartitionSpec as P

HEAD_FEATS = 4096
MODEL_DIM = 7168


quintic_first = 3.4445
quintic_third = -4.775
quintic_fifth = 2.0315


def shards(iterate):
    column_panel = lax.all_gather(iterate, "row", axis=0, tiled=True)
    gram_local = lax.psum_scatter(
        lax.dot_general(
            column_panel, iterate, (((1,), (1,)), ((), ())), preferred_element_type=jnp.float32
        ),
        "col",
        scatter_dimension=0,
        tiled=True,
    ).T
    gram_half = gram_local.astype(jnp.bfloat16)
    row_gram = lax.all_gather(gram_half, "col", axis=1, tiled=True)
    square = jnp.dot(
        row_gram,
        lax.all_gather(gram_half, "row", axis=0, tiled=True),
        preferred_element_type=jnp.float32,
    )
    poly = (quintic_third * gram_local + quintic_fifth * square).astype(jnp.bfloat16)
    mixed = jnp.dot(
        lax.all_gather(poly, "col", axis=1, tiled=True),
        column_panel,
        preferred_element_type=jnp.float32,
    )
    factor = 0.2 * math.sqrt(max(HEAD_FEATS, MODEL_DIM))
    update = factor * (quintic_first * iterate.astype(jnp.float32) + mixed)
    return update.astype(jnp.bfloat16)


def solution(mesh):
    in_specs = (P(("grp", "row"), "col"),)
    out_specs = P(("grp", "row"), "col")
    return jax.shard_map(shards, mesh=mesh, in_specs=in_specs, out_specs=out_specs, check_vma=False)
```

profile of v0, /device:TPU:0, one launch (start us, length us, event | category | flops | bytes accessed | tf_op | source)
XLA Modules:
  0.0 891.3 jit_solution(12632125990078381040)
XLA Ops:
  6.5 0.0 all-gather.5.cloned.1.call-start
  6.5 0.7 all-gather.5.cloned.1.call-update
  7.3 0.0 reduce-scatter.2.cloned.1.call-start
  7.3 144.6 %all-gather.5.cloned.1.call-done = bf16[4096,1792]{1,0:T(8,128)(2,1)} async-done(((bf16[1024,1792]{1,0:T(8,128)(2,1)}), bf16[4096,1792]{1,0:T(8,128)(2,1)}) %all-gather.5.cloned.1.call-update) | async-done | bytes 14680080 | tf_op jit(solution)/shard_map/all_gather | solution.py:18
  151.9 21.9 %fusion.1 = f32[4096,1024]{1,0:T(8,128)} fusion(bf16[4096,1792]{1,0:T(8,128)(2,1)} %all-gather.5.cloned.1.call-done, bf16[1024,1792]{1,0:T(8,128)(2,1)} %param.1), kind=kOutput, calls=%fused_computation.4 | convolution fusion | flops 15032385536 | bytes 35127296 | tf_op jit(solution)/shard_map/dot_general | solution.py:20
  173.8 0.0 reduce-scatter.2.cloned.1.call-update
  173.8 0.0 all-gather.7.cloned.1.call-start
  173.8 280.4 %reduce-scatter.2.cloned.1.call-done = f32[1024,1024]{1,0:T(8,128)} async-done(((f32[4096,1024]{1,0:T(8,128)}), f32[1024,1024]{1,0:T(8,128)}) %reduce-scatter.2.cloned.1.call-update) | async-done | bytes 4194320 | tf_op jit(solution)/shard_map/reduce_scatter | solution.py:19
  454.2 3.8 convert_bitcast_fusion
  458.1 0.0 all-gather.7.cloned.1.call-update
  458.1 0.0 all-gather.9.cloned.1.call-start
  458.1 0.5 all-gather.9.cloned.1.call-update
  458.7 0.0 all-gather.11.cloned.1.call-start
  458.7 149.9 %all-gather.7.cloned.1.call-done = bf16[1024,4096]{0,1:T(8,128)(2,1)} async-done(((bf16[1024,1024]{0,1:T(8,128)(2,1)}), bf16[1024,4096]{0,1:T(8,128)(2,1)}) %all-gather.7.cloned.1.call-update) | async-done | bytes 8388624 | tf_op jit(solution)/shard_map/all_gather | solution.py:28
  608.6 87.7 %all-gather.9.cloned.1.call-done = bf16[4096,1024]{0,1:T(8,128)(2,1)} async-done(((bf16[1024,1024]{0,1:T(8,128)(2,1)}), bf16[4096,1024]{0,1:T(8,128)(2,1)}) %all-gather.9.cloned.1.call-update) | async-done | bytes 8388624 | tf_op jit(solution)/shard_map/all_gather | solution.py:31
  696.3 15.3 %fusion = bf16[1024,1024]{0,1:T(8,128)(2,1)} fusion(f32[1024,1024]{1,0:T(8,128)} %reduce-scatter.2.cloned.1.call-done, bf16[4096,1024]{0,1:T(8,128)(2,1)} %all-gather.9.cloned.1.call-done, bf16[1024,4096]{0,1:T(8,128)(2,1)} %all-gather.7.cloned.1.call-done), kind=kOutput, calls=%fused_computation.2 | convolution fusion | flops 8594128896 | bytes 23068672 | tf_op jit(solution)/shard_map/dot_general | solution.py:29
  711.7 0.0 all-gather.11.cloned.1.call-update
  711.7 149.8 %all-gather.11.cloned.1.call-done = bf16[1024,4096]{0,1:T(8,128)(2,1)} async-done(((bf16[1024,1024]{0,1:T(8,128)(2,1)}), bf16[1024,4096]{0,1:T(8,128)(2,1)}) %all-gather.11.cloned.1.call-update) | async-done | bytes 8388624 | tf_op jit(solution)/shard_map/all_gather | solution.py:36
  861.5 23.3 %multiply_convert_fusion = bf16[1024,1792]{1,0:T(8,128)(2,1)} fusion(bf16[1024,1792]{1,0:T(8,128)(2,1)} %param.1, bf16[1024,4096]{0,1:T(8,128)(2,1)} %all-gather.11.cloned.1.call-done, bf16[4096,1792]{1,0:T(8,128)(2,1)} %all-gather.5.cloned.1.call-done), kind=kOutput, calls=%fused_computation | convolution fusion | flops 15041560576 | bytes 30408704 | tf_op jit(solution)/shard_map/dot_general | solution.py:35
Async XLA Ops:
  6.5 145.4 %all-gather.5.cloned.1.call-start = ((), (), s32[]{:S(2)}) async-start(), calls=%async_computation.1 | async-start | bytes 18350080 | tf_op jit(solution)/shard_map/all_gather | solution.py:18
  7.3 447.0 %reduce-scatter.2.cloned.1.call-start = ((), (), s32[]{:S(2)}) async-start(), calls=%async_computation.2 | async-start | bytes 20971520 | tf_op jit(solution)/shard_map/reduce_scatter | solution.py:19
  173.8 434.8 %all-gather.7.cloned.1.call-start = ((), (), s32[]{:S(2)}) async-start(), calls=%async_computation.3 | async-start | bytes 10485760 | tf_op jit(solution)/shard_map/all_gather | solution.py:28
  458.1 238.2 %all-gather.9.cloned.1.call-start = ((), (), s32[]{:S(2)}) async-start(), calls=%async_computation.4 | async-start | bytes 10485760 | tf_op jit(solution)/shard_map/all_gather | solution.py:31
  458.7 402.8 %all-gather.11.cloned.1.call-start = ((), (), s32[]{:S(2)}) async-start(), calls=%async_computation.5 | async-start | bytes 10485760 | tf_op jit(solution)/shard_map/all_gather | solution.py:36
Sparse Core Ops, SparseCore 0:
  9.2 142.6 all-gather.4
  173.9 280.2 reduce-scatter.1
  458.2 150.3 all-gather.6
  610.5 85.8 all-gather.8
  711.8 149.6 all-gather.10
where the time goes:
time: 891 us
  waiting for transfers between devices  814 us (91%)
  matrix products  60.5 us (7%)
  between operations  13.1 us (1%)
    reduce_scatter x1, waiting for transfers between devices, shards(): lax.psum_scatter(lax.dot_general(column_panel, iterate, (((1,), (1,)), ((...  280 us
    all_gather x1, waiting for transfers between devices, shards(): row_gram = lax.all_gather(gram_half, 'col', axis=1, tiled=True)  150 us
    all_gather x1, waiting for transfers between devices, shards(): lax.all_gather(poly, 'col', axis=1, tiled=True)  150 us
    all_gather x1, waiting for transfers between devices, shards(): column_panel = lax.all_gather(iterate, 'row', axis=0, tiled=True)  145 us
    all_gather x1, waiting for transfers between devices, shards(): lax.all_gather(gram_half, 'row', axis=0, tiled=True)  87.7 us
    dot_general x1, matrix products, shards(): jnp.dot(lax.all_gather(poly, 'col', axis=1, tiled=True), column_panel, pr...  23.3 us
    dot_general x1, matrix products, shards(): lax.dot_general(column_panel, iterate, (((1,), (1,)), ((), ())), preferre...  21.9 us
  transfers between devices with their start and end apart: 5, of which 5 were waited for; matrix products, arithmetic and copies ran while one was open for 0% of the time, Pallas kernels for 0%

commit v1 on v0

v1 whole, which is shorter than its diff:
```python
import math

import jax
import jax.numpy as jnp
from jax import lax
from jax.sharding import PartitionSpec as P

HEAD_FEATS = 4096
MODEL_DIM = 7168


quintic_first = 3.4445
quintic_third = -4.775
quintic_fifth = 2.0315

ROW_SETS = 2
PANELS = 2


def shards(iterate):
    rows, feats = iterate.shape
    sets = []
    for s in range(ROW_SETS):
        take = rows // ROW_SETS
        block = lax.all_gather(iterate[s * take : (s + 1) * take], "row", axis=0, tiled=True)
        partial = lax.dot_general(
            block, iterate, (((1,), (1,)), ((), ())), preferred_element_type=jnp.float32
        ).astype(jnp.bfloat16)
        owned = lax.psum_scatter(partial, "col", scatter_dimension=0, tiled=True)
        gram = lax.all_gather(owned, "col", axis=0, tiled=True)
        sets.append((block, gram))
    panel = jnp.concatenate([block for block, _ in sets], axis=0)
    gram_rows = jnp.concatenate([gram for _, gram in sets], axis=0).T
    factor = 0.2 * math.sqrt(max(HEAD_FEATS, MODEL_DIM))
    take = rows // ROW_SETS
    updates = []
    for p in range(PANELS):
        width = feats // PANELS
        columns = slice(p * width, (p + 1) * width)
        own = iterate[:, columns].astype(jnp.float32)
        once = jnp.dot(gram_rows, panel[:, columns], preferred_element_type=jnp.float32)
        inner = (quintic_third * own + quintic_fifth * once).astype(jnp.bfloat16)
        gathered = jnp.concatenate(
            [
                lax.all_gather(inner[s * take : (s + 1) * take], "row", axis=0, tiled=True)
                for s in range(ROW_SETS)
            ],
            axis=0,
        )
        mixed = jnp.dot(gram_rows, gathered, preferred_element_type=jnp.float32)
        updates.append((factor * (quintic_first * own + mixed)).astype(jnp.bfloat16))
    return jnp.concatenate(updates, axis=1)


def solution(mesh):
    in_specs = (P(("grp", "row"), "col"),)
    out_specs = P(("grp", "row"), "col")
    return jax.shard_map(shards, mesh=mesh, in_specs=in_specs, out_specs=out_specs, check_vma=False)
```

time: 891 us -> 736 us (0.83)
  waiting for transfers between devices: 814 us -> 608 us
  local copies, waits for them, and re-layouts: 0 us -> 30 us
  matrix products: 60.5 us -> 81.2 us
    reduce_scatter x1 -> x2, waiting for transfers between devices: 280 us -> 145 us  [shards(): owned = lax.psum_scatter(partial, 'col', scatter_dimension=0, tiled=True)]
    all_gather x4 -> x8, waiting for transfers between devices: 532 us -> 461 us  [the longest x4 167 us: shards(): lax.all_gather(inner[s * take:(s + 1) * take], 'row', axis=0, tiled=True)]
    dot_general x3 -> x6, matrix products: 60.5 us -> 81.2 us  [the longest x2 27.6 us: shards(): mixed = jnp.dot(gram_rows, gathered, preferred_element_type=jnp.float32)]
    concatenate x0 -> x2, local copies, waits for them, and re-layouts: none -> 11.9 us  [the longest x1 7.05 us: shards(): panel = jnp.concatenate([block for block, _ in sets], axis=0)]
    unnamed x0 -> x4, local copies, waits for them, and re-layouts: none -> 11.1 us
  transfers between devices with their start and end apart: 5 -> 10, of which waited for: 5 -> 10; matrix products, arithmetic and copies ran while one was open for 0% -> 10% of each run, Pallas kernels for 0% -> 0%
where the time goes in v1:
time: 736 us; the launch traced here: 735 us
  waiting for transfers between devices  608 us (83%)
  matrix products  81.2 us (11%)
  local copies, waits for them, and re-layouts  30 us (4%)
  between operations  13.6 us (2%)
    all_gather x4, waiting for transfers between devices, shards(): lax.all_gather(inner[s * take:(s + 1) * take], 'row', axis=0, tiled=True)  167 us
    all_gather x2, waiting for transfers between devices, shards(): lax.all_gather(iterate[s * take:(s + 1) * take], 'row', axis=0, tiled=True)  149 us
    reduce_scatter x2, waiting for transfers between devices, shards(): owned = lax.psum_scatter(partial, 'col', scatter_dimension=0, tiled=True)  145 us
    all_gather x2, waiting for transfers between devices, shards(): gram = lax.all_gather(owned, 'col', axis=0, tiled=True)  145 us
    dot_general x2, matrix products, shards(): mixed = jnp.dot(gram_rows, gathered, preferred_element_type=jnp.float32)  27.6 us
    dot_general x2, matrix products, shards(): jnp.dot(gram_rows, panel[:, columns], preferred_element_type=jnp.float32)  27.3 us
    dot_general x2, matrix products, shards(): lax.dot_general(block, iterate, (((1,), (1,)), ((), ())), preferred_eleme...  26.3 us
  transfers between devices with their start and end apart: 10, of which 10 were waited for; matrix products, arithmetic and copies ran while one was open for 10% of the time, Pallas kernels for 0%

profile of v1, /device:TPU:0, one launch (start us, length us, event | category | flops | bytes accessed | tf_op | source)
XLA Modules:
  0.0 735.4 jit_solution(10324017434272412345)
XLA Ops:
  6.5 0.0 all-gather.9.cloned.1.call-start
  6.5 4.1 fusion.32
  10.7 0.0 all-gather.9.cloned.1.call-update
  10.7 0.0 all-gather.13.cloned.1.call-start
  10.8 0.7 all-gather.13.cloned.1.call-update
  11.5 0.0 reduce-scatter.3.cloned.1.call-start
  11.5 80.9 %all-gather.9.cloned.1.call-done = bf16[2048,1792]{1,0:T(8,128)(2,1)} async-done(((bf16[512,1792]{1,0:T(8,128)(2,1)}), bf16[2048,1792]{1,0:T(8,128)(2,1)}) %all-gather.9.cloned.1.call-update) | async-done | bytes 7340048 | tf_op jit(solution)/shard_map/all_gather | solution.py:25
  92.4 13.1 %convolution_convert_fusion.1 = bf16[2048,1024]{1,0:T(8,128)(2,1)} fusion(bf16[2048,1792]{1,0:T(8,128)(2,1)} %all-gather.9.cloned.1.call-done, bf16[1024,1792]{1,0:T(8,128)(2,1)} %param.1), kind=kOutput, calls=%fused_computation.17 | convolution fusion | flops 7518289920 | bytes 15204352 | tf_op jit(solution)/shard_map/dot_general | solution.py:26
  105.5 0.0 reduce-scatter.3.cloned.1.call-update
  105.6 0.0 reduce-scatter.5.cloned.1.call-start
  105.6 67.6 %all-gather.13.cloned.1.call-done = bf16[2048,1792]{1,0:T(8,128)(2,1)} async-done(((bf16[512,1792]{1,0:T(8,128)(2,1)}), bf16[2048,1792]{1,0:T(8,128)(2,1)}) %all-gather.13.cloned.1.call-update) | async-done | bytes 7340048 | tf_op jit(solution)/shard_map/all_gather | solution.py:25
  173.2 13.2 %convolution_convert_fusion = bf16[2048,1024]{1,0:T(8,128)(2,1)} fusion(bf16[2048,1792]{1,0:T(8,128)(2,1)} %all-gather.13.cloned.1.call-done, bf16[1024,1792]{1,0:T(8,128)(2,1)} %param.1), kind=kOutput, calls=%fused_computation.16 | convolution fusion | flops 7518289920 | bytes 15204352 | tf_op jit(solution)/shard_map/dot_general | solution.py:26
  186.4 0.0 reduce-scatter.5.cloned.1.call-update
  186.4 0.0 all-gather.11.cloned.1.call-start
  186.4 65.9 %reduce-scatter.3.cloned.1.call-done = bf16[512,1024]{1,0:T(8,128)(2,1)} async-done(((bf16[2048,1024]{1,0:T(8,128)(2,1)}), bf16[512,1024]{1,0:T(8,128)(2,1)}) %reduce-scatter.3.cloned.1.call-update) | async-done | bytes 1048592 | tf_op jit(solution)/shard_map/reduce_scatter | solution.py:29
  252.3 0.0 all-gather.11.cloned.1.call-update
  252.3 0.0 all-gather.15.cloned.1.call-start
  252.4 79.5 %reduce-scatter.5.cloned.1.call-done = bf16[512,1024]{1,0:T(8,128)(2,1)} async-done(((bf16[2048,1024]{1,0:T(8,128)(2,1)}), bf16[512,1024]{1,0:T(8,128)(2,1)}) %reduce-scatter.5.cloned.1.call-update) | async-done | bytes 1048592 | tf_op jit(solution)/shard_map/reduce_scatter | solution.py:29
  331.9 0.0 all-gather.15.cloned.1.call-update
  331.9 0.2 all-gather.21.cloned.1.call-start
  332.1 6.5 constant_dynamic-update-slice_fusion.3
  338.6 7.0 constant_dynamic-update-slice_fusion.2
  345.6 68.9 %all-gather.11.cloned.1.call-done = bf16[2048,1024]{1,0:T(8,128)(2,1)} async-done(((bf16[512,1024]{1,0:T(8,128)(2,1)}), bf16[2048,1024]{1,0:T(8,128)(2,1)}) %all-gather.11.cloned.1.call-update) | async-done | bytes 4194320 | tf_op jit(solution)/shard_map/all_gather | solution.py:30
  414.6 4.6 constant_dynamic-update-slice_fusion.1
  419.2 76.2 %all-gather.15.cloned.1.call-done = bf16[2048,1024]{1,0:T(8,128)(2,1)} async-done(((bf16[512,1024]{1,0:T(8,128)(2,1)}), bf16[2048,1024]{1,0:T(8,128)(2,1)}) %all-gather.15.cloned.1.call-update) | async-done | bytes 4194320 | tf_op jit(solution)/shard_map/all_gather | solution.py:30
  495.3 0.0 copy-start
  495.3 4.8 constant_dynamic-update-slice_fusion
  500.1 0.0 copy-done
  500.1 13.5 %fusion.21 = bf16[1024,896]{1,0:T(8,128)(2,1)S(1)} fusion(bf16[4096,1024]{1,0:T(8,128)(2,1)} %constant_dynamic-update-slice_fusion, bf16[4096,1792]{1,0:T(8,128)(2,1)} %constant_dynamic-update-slice_fusion.2, bf16[1024,1792]{1,0:T(8,128)(2,1)S(1)} %copy-done), kind=kOutput, calls=%fused_computation.27 | convolution fusion | flops 7520780288 | bytes 19398656 | tf_op jit(solution)/shard_map/dot_general | solution.py:41
  513.7 1.4 fusion.34
  515.1 0.0 all-gather.21.cloned.1.call-update
  515.1 0.0 all-gather.23.cloned.1.call-start
  515.1 0.7 all-gather.23.cloned.1.call-update
  515.8 0.0 all-gather.17.cloned.1.call-start
  515.9 13.8 %fusion.16 = bf16[1024,896]{1,0:T(8,128)(2,1)S(1)} fusion(bf16[4096,1024]{1,0:T(8,128)(2,1)} %constant_dynamic-update-slice_fusion, bf16[4096,1792]{1,0:T(8,128)(2,1)} %constant_dynamic-update-slice_fusion.2, bf16[1024,1792]{1,0:T(8,128)(2,1)} %param.1), kind=kOutput, calls=%fused_computation.22 | convolution fusion | flops 7520780288 | bytes 19398656 | tf_op jit(solution)/shard_map/dot_general | solution.py:41
  529.7 1.5 fusion.33
  531.2 0.0 all-gather.17.cloned.1.call-update
  531.2 0.3 all-gather.19.cloned.1.call-start
  531.5 0.3 all-gather.19.cloned.1.call-update
  531.8 30.3 %all-gather.21.cloned.1.call-done = bf16[2048,896]{1,0:T(8,128)(2,1)} async-done(((bf16[512,896]{1,0:T(8,128)(2,1)}), bf16[2048,896]{1,0:T(8,128)(2,1)}) %all-gather.21.cloned.1.call-update) | async-done | bytes 3670032 | tf_op jit(solution)/shard_map/all_gather | solution.py:45
  562.1 50.2 %all-gather.23.cloned.1.call-done = bf16[2048,896]{1,0:T(8,128)(2,1)} async-done(((bf16[512,896]{1,0:T(8,128)(2,1)}), bf16[2048,896]{1,0:T(8,128)(2,1)}) %all-gather.23.cloned.1.call-update) | async-done | bytes 3670032 | tf_op jit(solution)/shard_map/all_gather | solution.py:45
  612.3 13.8 %fusion.19 = bf16[1024,896]{1,0:T(8,128)(2,1)S(1)} fusion(bf16[4096,1024]{1,0:T(8,128)(2,1)} %constant_dynamic-update-slice_fusion, bf16[2048,896]{1,0:T(8,128)(2,1)} %all-gather.23.cloned.1.call-done, bf16[2048,896]{1,0:T(8,128)(2,1)} %all-gather.21.cloned.1.call-done, bf16[1024,1792]{1,0:T(8,128)(2,1)} %param.1), kind=kOutput, calls=%fused_computation.25 | convolution fusion | flops 7535460352 | bytes 19398656 | tf_op jit(solution)/shard_map/dot_general | solution.py:50
  626.1 36.4 %all-gather.17.cloned.1.call-done = bf16[2048,896]{1,0:T(8,128)(2,1)} async-done(((bf16[512,896]{1,0:T(8,128)(2,1)}), bf16[2048,896]{1,0:T(8,128)(2,1)}) %all-gather.17.cloned.1.call-update) | async-done | bytes 3670032 | tf_op jit(solution)/shard_map/all_gather | solution.py:45
  662.6 50.1 %all-gather.19.cloned.1.call-done = bf16[2048,896]{1,0:T(8,128)(2,1)} async-done(((bf16[512,896]{1,0:T(8,128)(2,1)}), bf16[2048,896]{1,0:T(8,128)(2,1)}) %all-gather.19.cloned.1.call-update) | async-done | bytes 3670032 | tf_op jit(solution)/shard_map/all_gather | solution.py:45
  712.6 13.8 %fusion.14 = bf16[1024,896]{1,0:T(8,128)(2,1)S(1)} fusion(bf16[4096,1024]{1,0:T(8,128)(2,1)} %constant_dynamic-update-slice_fusion, bf16[2048,896]{1,0:T(8,128)(2,1)} %all-gather.19.cloned.1.call-done, bf16[2048,896]{1,0:T(8,128)(2,1)} %all-gather.17.cloned.1.call-done, bf16[1024,1792]{1,0:T(8,128)(2,1)} %param.1), kind=kOutput, calls=%fused_computation.20 | convolution fusion | flops 7535460352 | bytes 19398656 | tf_op jit(solution)/shard_map/dot_general | solution.py:50
  726.4 2.1 pad_maximum_fusion
Async XLA Ops:
  6.5 85.9 %all-gather.9.cloned.1.call-start = ((), (), s32[]{:S(2)}) async-start(), calls=%async_computation.2 | async-start | bytes 9175040 | tf_op jit(solution)/shard_map/all_gather | solution.py:25
  10.7 162.5 %all-gather.13.cloned.1.call-start = ((), (), s32[]{:S(2)}) async-start(), calls=%async_computation.5 | async-start | bytes 9175040 | tf_op jit(solution)/shard_map/all_gather | solution.py:25
  11.5 240.8 %reduce-scatter.3.cloned.1.call-start = ((), (), s32[]{:S(2)}) async-start(), calls=%async_computation.3 | async-start | bytes 5242880 | tf_op jit(solution)/shard_map/reduce_scatter | solution.py:29
  105.6 226.3 %reduce-scatter.5.cloned.1.call-start = ((), (), s32[]{:S(2)}) async-start(), calls=%async_computation.6 | async-start | bytes 5242880 | tf_op jit(solution)/shard_map/reduce_scatter | solution.py:29
  186.4 228.2 %all-gather.11.cloned.1.call-start = ((), (), s32[]{:S(2)}) async-start(), calls=%async_computation.4 | async-start | bytes 5242880 | tf_op jit(solution)/shard_map/all_gather | solution.py:30
  252.3 243.0 %all-gather.15.cloned.1.call-start = ((), (), s32[]{:S(2)}) async-start(), calls=%async_computation.7 | async-start | bytes 5242880 | tf_op jit(solution)/shard_map/all_gather | solution.py:30
  331.9 230.2 %all-gather.21.cloned.1.call-start = ((), (), s32[]{:S(2)}) async-start(), calls=%async_computation.10 | async-start | bytes 4587520 | tf_op jit(solution)/shard_map/all_gather | solution.py:45
  495.3 4.8 copy-start
  515.1 97.2 %all-gather.23.cloned.1.call-start = ((), (), s32[]{:S(2)}) async-start(), calls=%async_computation.11 | async-start | bytes 4587520 | tf_op jit(solution)/shard_map/all_gather | solution.py:45
  515.8 146.7 %all-gather.17.cloned.1.call-start = ((), (), s32[]{:S(2)}) async-start(), calls=%async_computation.8 | async-start | bytes 4587520 | tf_op jit(solution)/shard_map/all_gather | solution.py:45
  531.2 181.4 %all-gather.19.cloned.1.call-start = ((), (), s32[]{:S(2)}) async-start(), calls=%async_computation.9 | async-start | bytes 4587520 | tf_op jit(solution)/shard_map/all_gather | solution.py:45
Sparse Core Ops, SparseCore 0:
  10.8 81.5 all-gather.8
  94.3 78.8 all-gather.12
  175.5 76.7 reduce-scatter.2
  254.6 77.2 reduce-scatter.4
  333.3 81.2 all-gather.10
  416.0 79.2 all-gather.14
  515.2 46.8 all-gather.20
  564.0 48.3 all-gather.22
  614.2 48.3 all-gather.16
  664.3 48.3 all-gather.18

commit v2 on v0

v2 whole, which is shorter than its diff:
```python
import math

import jax
import jax.numpy as jnp
from jax import lax
from jax.sharding import PartitionSpec as P

HEAD_FEATS = 4096
MODEL_DIM = 7168


quintic_first = 3.4445
quintic_third = -4.775
quintic_fifth = 2.0315


def swap(block, offset, count):
    return lax.ppermute(block, "row", [(i, i ^ offset) for i in range(count)])


def gather_blocks(block, count):
    half = block.shape[0] // 2
    blocks = [block]
    for offset in range(1, count):
        top = 1 << (offset.bit_length() - 1)
        low = offset & -offset
        if top == offset:
            blocks.append(swap(block, offset, count))
        else:
            first = swap(blocks[offset ^ top][:half], top, count)
            second = swap(blocks[offset ^ low][half:], low, count)
            blocks.append(jnp.concatenate([first, second], axis=0))
    return blocks


def times_transpose(left, right):
    return lax.dot_general(
        left, right, (((1,), (1,)), ((), ())), preferred_element_type=jnp.float32
    )


def sum_over_columns(partial):
    owned = lax.psum_scatter(partial.astype(jnp.bfloat16), "col", scatter_dimension=0, tiled=True)
    return lax.all_gather(owned, "col", axis=0, tiled=True)


def shards(iterate):
    count = lax.axis_size("row")
    rows = iterate.shape[0]
    half = rows // 2
    me = lax.axis_index("row")
    wide = iterate.astype(jnp.float32)
    blocks = gather_blocks(iterate, count)

    diagonal = lax.psum(jnp.sum(wide * wide, axis=1, keepdims=True), "col")
    eye = lax.broadcasted_iota(jnp.int32, (rows, rows), 0) == lax.broadcasted_iota(
        jnp.int32, (rows, rows), 1
    )
    gram = [sum_over_columns(jnp.where(eye, 0.0, times_transpose(iterate, iterate)))]
    for offset in range(1, count):
        lower = (me & (1 << (offset.bit_length() - 1))) == 0
        other = blocks[offset]
        tall = jnp.where(lower, iterate, other)
        short = jnp.where(lower, other[:half], iterate[half:])
        mine = sum_over_columns(times_transpose(short, tall))
        theirs = swap(mine, offset, count)
        pair = jnp.concatenate(
            [jnp.where(lower, mine, theirs), jnp.where(lower, theirs, mine)], axis=0
        )
        gram.append(jnp.where(lower, pair.T, pair))

    def apply_gram(own, parts):
        total = diagonal * own
        for block, part in zip(gram, parts):
            total = total + jnp.dot(block, part, preferred_element_type=jnp.float32)
        return total

    inner = quintic_third * wide + quintic_fifth * apply_gram(wide, blocks)
    mixed = apply_gram(inner, gather_blocks(inner.astype(jnp.bfloat16), count))
    factor = 0.2 * math.sqrt(max(HEAD_FEATS, MODEL_DIM))
    return (factor * (quintic_first * wide + mixed)).astype(jnp.bfloat16)


def solution(mesh):
    in_specs = (P(("grp", "row"), "col"),)
    out_specs = P(("grp", "row"), "col")
    return jax.shard_map(shards, mesh=mesh, in_specs=in_specs, out_specs=out_specs, check_vma=False)
```

time: 891 us -> 553 us (0.62)
  waiting for transfers between devices: 814 us -> 374 us
  matrix products: 60.5 us -> 105 us
  local copies, waits for them, and re-layouts: 0 us -> 22.1 us
  starting transfers between devices: 0.16 us -> 19.3 us
  blocking collectives: 0 us -> 10.3 us
    all_gather x4, waiting for transfers between devices: 532 us -> 94 us  [sum_over_columns(): return lax.all_gather(owned, 'col', axis=0, tiled=True)]
    reduce_scatter x1 -> x4, waiting for transfers between devices: 280 us -> 81.8 us  [sum_over_columns(): lax.psum_scatter(partial.astype(jnp.bfloat16), 'col', scatter_dimension=0...]
    ppermute x0 -> x11, waiting for transfers between devices: none -> 198 us  [swap(): return lax.ppermute(block, 'row', [(i, i ^ offset) for i in range(count)])]
    dot_general x3 -> x12, matrix products: 60.5 us -> 105 us  [the longest x8 80.9 us: apply_gram(): total = total + jnp.dot(block, part, preferred_element_type=jnp.float32)]
    ppermute x0 -> x11, starting transfers between devices: none -> 19 us  [swap(): return lax.ppermute(block, 'row', [(i, i ^ offset) for i in range(count)])]
    psum x0 -> x1, blocking collectives: none -> 10.3 us  [shards(): diagonal = lax.psum(jnp.sum(wide * wide, axis=1, keepdims=True), 'col')]
  transfers between devices with their start and end apart: 5 -> 19, of which waited for: 5 -> 15; matrix products, arithmetic and copies ran while one was open for 0% -> 17% of each run, Pallas kernels for 0% -> 0%
where the time goes in v2:
time: 553 us; the launch traced here: 552 us
  waiting for transfers between devices  374 us (68%)
  matrix products  105 us (19%)
  local copies, waits for them, and re-layouts  22.1 us (4%)
  starting transfers between devices  19.3 us (3%)
  between operations  13.7 us (2%)
  blocking collectives  10.3 us (2%)
  other arithmetic  7.8 us (1%)
    ppermute x11, waiting for transfers between devices, swap(): return lax.ppermute(block, 'row', [(i, i ^ offset) for i in range(count)])  198 us
    all_gather x4, waiting for transfers between devices, sum_over_columns(): return lax.all_gather(owned, 'col', axis=0, tiled=True)  94 us
    reduce_scatter x4, waiting for transfers between devices, sum_over_columns(): lax.psum_scatter(partial.astype(jnp.bfloat16), 'col', scatter_dimension=0...  81.8 us
    dot_general x8, matrix products, apply_gram(): total = total + jnp.dot(block, part, preferred_element_type=jnp.float32)  80.9 us
    dot_general x4, matrix products, times_transpose(): lax.dot_general(left, right, (((1,), (1,)), ((), ())), preferred_element_...  24.2 us
    ppermute x11, starting transfers between devices, swap(): return lax.ppermute(block, 'row', [(i, i ^ offset) for i in range(count)])  19 us
  transfers between devices with their start and end apart: 19, of which 15 were waited for; matrix products, arithmetic and copies ran while one was open for 17% of the time, Pallas kernels for 0%

profile of v2, /device:TPU:0, one launch (start us, length us, event | category | flops | bytes accessed | tf_op | source)
XLA Modules:
  0.0 552.3 jit_solution(789146847977734065)
XLA Ops:
  6.5 3.0 collective-permute-start.2
  9.5 1.5 collective-permute-start
  11.0 78.2 %collective-permute-done.2 = bf16[1024,1792]{1,0:T(8,128)(2,1)} collective-permute-done((bf16[1024,1792]{1,0:T(8,128)(2,1)}, bf16[1024,1792]{1,0:T(8,128)(2,1)}, u32[]{:S(2)}, u32[]{:S(2)}) %collective-permute-start.2) | collective-permute-done | bytes 3670048 | tf_op jit(solution)/shard_map/ppermute | solution.py:18
  89.2 6.2 %fusion.35 = bf16[512,1024]{1,0:T(8,128)(2,1)} fusion(bf16[1024,1792]{1,0:T(8,128)(2,1)} %param.1, bf16[1024,1792]{1,0:T(8,128)(2,1)} %collective-permute-done.2, pred[]{:T(512)S(6)} %eq.12), kind=kOutput, calls=%fused_computation.42 | convolution fusion | flops 1882324992 | bytes 12059648 | tf_op jit(solution)/shard_map/dot_general | solution.py:37
  95.4 0.0 reduce-scatter.7.cloned.1.call-start
  95.5 6.2 %fusion.30 = bf16[512,1024]{1,0:T(8,128)(2,1)} fusion(bf16[1024,1792]{1,0:T(8,128)(2,1)} %param.1, bf16[1024,1792]{1,0:T(8,128)(2,1)} %collective-permute-done, pred[]{:T(512)S(6)} %eq.11), kind=kOutput, calls=%fused_computation.41 | convolution fusion | flops 1882324992 | bytes 12059648 | tf_op jit(solution)/shard_map/dot_general | solution.py:37
  101.7 0.0 reduce-scatter.5.cloned.1.call-start
  101.8 8.6 %select_convert_fusion = bf16[1024,1024]{1,0:T(8,128)(2,1)} fusion(bf16[1024,1792]{1,0:T(8,128)(2,1)} %param.1), kind=kOutput, calls=%fused_computation.14 | convolution fusion | flops 3761242112 | bytes 5767168 | tf_op jit(solution)/shard_map/dot_general | solution.py:37
  110.4 0.0 all-gather.9.cloned.1.call-start
  110.5 2.9 slice.27
  113.3 1.7 collective-permute-start.4
  115.1 9.1 %reduce-scatter.9.cloned.1.call-done = bf16[128,1024]{1,0:T(8,128)(2,1)} async-done(((bf16[512,1024]{1,0:T(8,128)(2,1)}), bf16[128,1024]{1,0:T(8,128)(2,1)}) %reduce-scatter.9.cloned.1.call-update) | async-done | bytes 262160 | tf_op jit(solution)/shard_map/reduce_scatter | solution.py:43
  124.3 2.9 slice.29
  127.1 1.5 collective-permute-start.5
  128.6 23.8 %reduce-scatter.7.cloned.1.call-done = bf16[128,1024]{1,0:T(8,128)(2,1)} async-done(((bf16[512,1024]{1,0:T(8,128)(2,1)}), bf16[128,1024]{1,0:T(8,128)(2,1)}) %reduce-scatter.7.cloned.1.call-update) | async-done | bytes 262160 | tf_op jit(solution)/shard_map/reduce_scatter | solution.py:43
  152.5 2.2 collective-permute-done.4
  154.7 0.1 constant_dynamic-update-slice_fusion.1
  154.9 14.2 %collective-permute-done.5 = bf16[512,1792]{1,0:T(8,128)(2,1)} collective-permute-done((bf16[512,1792]{1,0:T(8,128)(2,1)}, bf16[512,1792]{1,0:T(8,128)(2,1)}, u32[]{:S(2)}, u32[]{:S(2)}) %collective-permute-start.5) | collective-permute-done | bytes 1835040 | tf_op jit(solution)/shard_map/ppermute | solution.py:18
  169.0 1.6 constant_dynamic-update-slice_fusion
  170.7 1.8 copy-done.2
  172.5 3.1 fusion.38
  175.7 21.6 %reduce-scatter.5.cloned.1.call-done = bf16[256,1024]{1,0:T(8,128)(2,1)} async-done(((bf16[1024,1024]{1,0:T(8,128)(2,1)}), bf16[256,1024]{1,0:T(8,128)(2,1)}) %reduce-scatter.5.cloned.1.call-update) | async-done | bytes 524304 | tf_op jit(solution)/shard_map/reduce_scatter | solution.py:43
  197.3 28.7 %all-gather.9.cloned.1.call-done = bf16[512,1024]{1,0:T(8,128)(2,1)} async-done(((bf16[128,1024]{1,0:T(8,128)(2,1)}), bf16[512,1024]{1,0:T(8,128)(2,1)}) %all-gather.9.cloned.1.call-update) | async-done | bytes 1048592 | tf_op jit(solution)/shard_map/all_gather | solution.py:44
  226.0 1.5 collective-permute-start.3
  227.5 2.8 fusion.3
  230.3 10.3 %psum.7 = f32[1024]{0:T(1024)S(1)} all-reduce(f32[1024]{0:T(1024)S(1)} %fusion.3), channel_id=1, replica_groups=mesh['grp'=2,'row'=4,'col'=4] {'col'}, use_global_device_ids=true, to_apply=%region_1.0 | all-reduce | flops 1024 | bytes 8192 | tf_op jit(solution)/shard_map/psum | solution.py:55
  240.6 14.5 %all-gather.7.cloned.1.call-done = bf16[512,1024]{1,0:T(8,128)(2,1)} async-done(((bf16[128,1024]{1,0:T(8,128)(2,1)}), bf16[512,1024]{1,0:T(8,128)(2,1)}) %all-gather.7.cloned.1.call-update) | async-done | bytes 1048592 | tf_op jit(solution)/shard_map/all_gather | solution.py:44
  255.1 1.5 collective-permute-start.1
  256.6 27.4 %reduce-scatter.11.cloned.1.call-done = bf16[128,1024]{1,0:T(8,128)(2,1)} async-done(((bf16[512,1024]{1,0:T(8,128)(2,1)}), bf16[128,1024]{1,0:T(8,128)(2,1)}) %reduce-scatter.11.cloned.1.call-update) | async-done | bytes 262160 | tf_op jit(solution)/shard_map/reduce_scatter | solution.py:43
  284.0 46.2 %all-gather.5.cloned.1.call-done = bf16[1024,1024]{1,0:T(8,128)(2,1)} async-done(((bf16[256,1024]{1,0:T(8,128)(2,1)}), bf16[1024,1024]{1,0:T(8,128)(2,1)}) %all-gather.5.cloned.1.call-update) | async-done | bytes 2097168 | tf_op jit(solution)/shard_map/all_gather | solution.py:44
  330.2 9.5 %fusion.56 = f32[1024,1792]{1,0:T(8,128)} fusion(bf16[1024,1024]{1,0:T(8,128)(2,1)} %all-gather.5.cloned.1.call-done, bf16[1024,1792]{1,0:T(8,128)(2,1)} %param.1), kind=kOutput, calls=%fused_computation.65 | convolution fusion | flops 3758096384 | bytes 13107200 | tf_op jit(solution)/shard_map/dot_general | solution.py:75
  339.7 0.1 broadcast_select_fusion.4
  339.8 1.0 copy-done.5
  340.8 0.3 pad_maximum_fusion.1
  341.1 2.6 copy.3
  343.7 10.1 %fusion.50 = f32[1024,1792]{1,0:T(8,128)} fusion(bf16[1024,1792]{1,0:T(8,128)(2,1)} %collective-permute-done.2, bf16[1024,1024]{0,1:T(8,128)(2,1)} %copy.3, pred[]{:T(512)S(6)} %eq.12, bf16[512,1024]{1,0:T(8,128)(2,1)} %copy-done.5, bf16[512,1024]{1,0:T(8,128)(2,1)S(1)} %get-tuple-element.9), kind=kOutput, calls=%fused_computation.57 | convolution fusion | flops 3763339264 | bytes 15204353 | tf_op jit(solution)/shard_map/dot_general | solution.py:75
  353.8 4.6 all-gather.11.cloned.1.call-done
  358.4 2.4 collective-permute-start.6
  360.8 1.4 broadcast_select_fusion.6
  362.2 1.0 copy-done.9
  363.2 0.3 pad_maximum_fusion
  363.5 2.6 copy.2
  366.0 10.0 %fusion.48 = f32[1024,1792]{1,0:T(8,128)} fusion(bf16[1024,1792]{1,0:T(8,128)(2,1)} %collective-permute-done, bf16[1024,1024]{0,1:T(8,128)(2,1)} %copy.2, pred[]{:T(512)S(6)} %eq.11, bf16[512,1024]{1,0:T(8,128)(2,1)} %copy-done.9, bf16[512,1024]{1,0:T(8,128)(2,1)S(1)} %get-tuple-element.7), kind=kOutput, calls=%fused_computation.55 | convolution fusion | flops 3763339264 | bytes 15204353 | tf_op jit(solution)/shard_map/dot_general | solution.py:75
  376.0 8.4 %collective-permute-done.6 = bf16[512,1024]{1,0:T(8,128)(2,1)} collective-permute-done((bf16[512,1024]{1,0:T(8,128)(2,1)}, bf16[512,1024]{1,0:T(8,128)(2,1)}, u32[]{:S(2)}, u32[]{:S(2)}) %collective-permute-start.6) | collective-permute-done | bytes 1048608 | tf_op jit(solution)/shard_map/ppermute | solution.py:18
  384.4 1.4 broadcast_select_fusion.2
  385.8 0.9 copy-done.1
  386.7 1.6 fusion.46
  388.3 2.9 copy.4
  391.1 14.6 %fusion.55 = (bf16[1024,1792]{1,0:T(8,128)(2,1)S(1)}, f32[1024,1792]{1,0:T(8,128)}) fusion(bf16[1024,1792]{1,0:T(8,128)(2,1)} %copy-done.2, bf16[1024,1024]{1,0:T(8,128)(2,1)S(1)} %copy.4, pred[]{:T(512)S(6)} %eq.12, bf16[512,1024]{1,0:T(8,128)(2,1)} %copy-done.1, bf16[512,1024]{1,0:T(8,128)(2,1)S(1)} %get-tuple-element.5, f32[1024,1792]{1,0:T(8,128)} %fusion.50, ...), kind=kOutput, calls=%fused_computation.64 | convolution fusion | flops 3781689344 | bytes 44568576 | tf_op jit(solution)/shard_map/dot_general | solution.py:75
  405.7 1.5 collective-permute-start.8
  407.2 1.5 collective-permute-start.7
  408.6 77.1 %collective-permute-done.8 = bf16[1024,1792]{1,0:T(8,128)(2,1)S(1)} collective-permute-done((bf16[1024,1792]{1,0:T(8,128)(2,1)S(1)}, bf16[1024,1792]{1,0:T(8,128)(2,1)S(1)}, u32[]{:S(2)}, u32[]{:S(2)}) %collective-permute-start.8) | collective-permute-done | bytes 3670048 | tf_op jit(solution)/shard_map/ppermute | solution.py:18
  485.7 0.1 slice.31
  485.9 1.5 collective-permute-start.10
  487.4 0.1 slice.30
  487.6 1.5 collective-permute-start.9
  489.1 6.0 %fusion.57 = f32[1024,1792]{1,0:T(8,128)} fusion(bf16[1024,1024]{1,0:T(8,128)(2,1)S(1)} %copy-done.18, bf16[1024,1792]{1,0:T(8,128)(2,1)S(1)} %get-tuple-element.11), kind=kOutput, calls=%fused_computation.66 | convolution fusion | flops 3758096384 | bytes 13107200 | tf_op jit(solution)/shard_map/dot_general | solution.py:75
  495.1 7.0 %fusion.49 = f32[1024,1792]{1,0:T(8,128)} fusion(bf16[1024,1792]{1,0:T(8,128)(2,1)S(1)} %collective-permute-done.8, bf16[1024,1024]{0,1:T(8,128)(2,1)S(1)} %copy-done.11, pred[]{:T(512)S(6)} %eq.12, bf16[512,1024]{1,0:T(8,128)(2,1)S(1)} %copy-done.6, bf16[512,1024]{1,0:T(8,128)(2,1)S(1)} %copy-done.4), kind=kOutput, calls=%fused_computation.56 | convolution fusion | flops 3763339264 | bytes 15204353 | tf_op jit(solution)/shard_map/dot_general | solution.py:75
  502.2 7.0 %fusion.47 = f32[1024,1792]{1,0:T(8,128)} fusion(bf16[1024,1792]{1,0:T(8,128)(2,1)S(1)} %collective-permute-done.7, bf16[1024,1024]{0,1:T(8,128)(2,1)S(1)} %copy-done.12, pred[]{:T(512)S(6)} %eq.11, bf16[512,1024]{1,0:T(8,128)(2,1)S(1)} %copy-done.10, bf16[512,1024]{1,0:T(8,128)(2,1)S(1)} %copy-done.8), kind=kOutput, calls=%fused_computation.54 | convolution fusion | flops 3763339264 | bytes 15204353 | tf_op jit(solution)/shard_map/dot_general | solution.py:75
  509.2 17.1 %collective-permute-done.10 = bf16[512,1792]{1,0:T(8,128)(2,1)S(1)} collective-permute-done((bf16[512,1792]{1,0:T(8,128)(2,1)S(1)}, bf16[512,1792]{1,0:T(8,128)(2,1)S(1)}, u32[]{:S(2)}, u32[]{:S(2)}) %collective-permute-start.10) | collective-permute-done | bytes 1835040 | tf_op jit(solution)/shard_map/ppermute | solution.py:18
  526.3 0.9 collective-permute-done.9
  527.1 0.4 copy-done.13
  527.5 1.2 copy-done.14
  528.7 16.7 %fusion.2 = bf16[1024,1792]{1,0:T(8,128)(2,1)} fusion(bf16[1024,1792]{1,0:T(8,128)(2,1)} %param.1, f32[1024,1792]{1,0:T(8,128)} %fusion.49, f32[1024,1792]{1,0:T(8,128)} %fusion.47, f32[1024,1792]{1,0:T(8,128)} %fusion.57, f32[1024,1792]{1,0:T(8,128)} %get-tuple-element.12, bf16[512,1792]{1,0:T(8,128)(2,1)} %copy-done.13, bf16[512,1792]{1,0:T(8,128)(2,1)} %copy-done.14, ...), kind=kOutput, calls=%fused_computation.6 | convolution fusion | flops 3789029376 | bytes 44568576 | tf_op jit(solution)/shard_map/dot_general | solution.py:75
  (49 shorter events, 0.4 us)
Async XLA Ops:
  6.5 117.7 %reduce-scatter.9.cloned.1.call-start = ((), (), s32[]{:S(2)}) async-start(), calls=%async_computation.8 | async-start | bytes 1310720 | tf_op jit(solution)/shard_map/reduce_scatter | solution.py:43
  6.5 82.6 %collective-permute-start.2 = (bf16[1024,1792]{1,0:T(8,128)(2,1)}, bf16[1024,1792]{1,0:T(8,128)(2,1)}, u32[]{:S(2)}, u32[]{:S(2)}) collective-permute-start(bf16[1024,1792]{1,0:T(8,128)(2,1)} %param.1), channel_id=1, source_target_pairs={{0,8},{4,12},{8,0},{12,4},{1,9},{5,13},{9,1},{13,5},{2,10},{6,14},... | collective-permute-start | bytes 11010056 | tf_op jit(solution)/shard_map/ppermute | solution.py:18
  9.5 86.0 %collective-permute-start = (bf16[1024,1792]{1,0:T(8,128)(2,1)}, bf16[1024,1792]{1,0:T(8,128)(2,1)}, u32[]{:S(2)}, u32[]{:S(2)}) collective-permute-start(bf16[1024,1792]{1,0:T(8,128)(2,1)} %param.1), channel_id=1, source_target_pairs={{0,4},{4,0},{8,12},{12,8},{1,5},{5,1},{9,13},{13,9},{2,6},{6,2},{1... | collective-permute-start | bytes 11010056 | tf_op jit(solution)/shard_map/ppermute | solution.py:18
  95.4 57.0 %reduce-scatter.7.cloned.1.call-start = ((), (), s32[]{:S(2)}) async-start(), calls=%async_computation.6 | async-start | bytes 1310720 | tf_op jit(solution)/shard_map/reduce_scatter | solution.py:43
  101.7 95.5 %reduce-scatter.5.cloned.1.call-start = ((), (), s32[]{:S(2)}) async-start(), calls=%async_computation.4 | async-start | bytes 2621440 | tf_op jit(solution)/shard_map/reduce_scatter | solution.py:43
  110.4 115.6 %all-gather.9.cloned.1.call-start = ((), (), s32[]{:S(2)}) async-start(), calls=%async_computation.9 | async-start | bytes 1310720 | tf_op jit(solution)/shard_map/all_gather | solution.py:44
  113.3 41.4 %collective-permute-start.4 = (bf16[512,1792]{1,0:T(8,128)(2,1)}, bf16[512,1792]{1,0:T(8,128)(2,1)S(1)}, u32[]{:S(2)}, u32[]{:S(2)}) collective-permute-start(bf16[512,1792]{1,0:T(8,128)(2,1)} %slice.27), channel_id=1, source_target_pairs={{0,8},{4,12},{8,0},{12,4},{1,9},{5,13},{9,1},{13,5},{2,10},{6,14},... | collective-permute-start | bytes 5505032 | tf_op jit(solution)/shard_map/ppermute | solution.py:18
  124.2 130.9 %all-gather.7.cloned.1.call-start = ((), (), s32[]{:S(2)}) async-start(), calls=%async_computation.7 | async-start | bytes 1310720 | tf_op jit(solution)/shard_map/all_gather | solution.py:44
  127.1 41.9 %collective-permute-start.5 = (bf16[512,1792]{1,0:T(8,128)(2,1)}, bf16[512,1792]{1,0:T(8,128)(2,1)}, u32[]{:S(2)}, u32[]{:S(2)}) collective-permute-start(bf16[512,1792]{1,0:T(8,128)(2,1)} %slice.29), channel_id=1, source_target_pairs={{0,4},{4,0},{8,12},{12,8},{1,5},{5,1},{9,13},{13,9},{2,6},{6,2},{1... | collective-permute-start | bytes 5505032 | tf_op jit(solution)/shard_map/ppermute | solution.py:18
  152.4 131.5 %reduce-scatter.11.cloned.1.call-start = ((), (), s32[]{:S(2)}) async-start(), calls=%async_computation.10 | async-start | bytes 1310720 | tf_op jit(solution)/shard_map/reduce_scatter | solution.py:43
  152.5 20.0 %copy-start = (bf16[1024,1792]{1,0:T(8,128)(2,1)S(1)}, bf16[1024,1792]{1,0:T(8,128)(2,1)}, u32[]{:S(2)}) copy-start(bf16[1024,1792]{1,0:T(8,128)(2,1)} %param.1) | copy-start | bytes 11010052
  170.6 1.8 copy-start.2
  175.6 154.5 %all-gather.5.cloned.1.call-start = ((), (), s32[]{:S(2)}) async-start(), calls=%async_computation.5 | async-start | bytes 2621440 | tf_op jit(solution)/shard_map/all_gather | solution.py:44
  197.3 161.1 %all-gather.11.cloned.1.call-start = ((), (), s32[]{:S(2)}) async-start(), calls=%async_computation.11 | async-start | bytes 1310720 | tf_op jit(solution)/shard_map/all_gather | solution.py:44
  226.0 113.6 %collective-permute-start.3 = (bf16[512,1024]{1,0:T(8,128)(2,1)}, bf16[512,1024]{1,0:T(8,128)(2,1)S(1)}, u32[]{:S(2)}, u32[]{:S(2)}) collective-permute-start(bf16[512,1024]{1,0:T(8,128)(2,1)} %all-gather.9.cloned.1.call-done), channel_id=1, source_target_pairs={{0,8},{4,12},{8,0},{12,4},{1,9},{5,13},{9,1},{13,5},{2,10},{6,14},... | collective-permute-start | bytes 3145736 | tf_op jit(solution)/shard_map/ppermute | solution.py:18
  255.1 105.7 %collective-permute-start.1 = (bf16[512,1024]{1,0:T(8,128)(2,1)}, bf16[512,1024]{1,0:T(8,128)(2,1)}, u32[]{:S(2)}, u32[]{:S(2)}) collective-permute-start(bf16[512,1024]{1,0:T(8,128)(2,1)} %all-gather.7.cloned.1.call-done), channel_id=1, source_target_pairs={{0,4},{4,0},{8,12},{12,8},{1,5},{5,1},{9,13},{13,9},{2,6},{6,2},{1... | collective-permute-start | bytes 3145736 | tf_op jit(solution)/shard_map/ppermute | solution.py:18
  284.0 55.7 %copy-start.16 = (bf16[512,1024]{1,0:T(8,128)(2,1)S(1)}, bf16[512,1024]{1,0:T(8,128)(2,1)}, u32[]{:S(2)}) copy-start(bf16[512,1024]{1,0:T(8,128)(2,1)} %all-gather.9.cloned.1.call-done) | copy-start | bytes 3145732
  339.8 1.0 copy-start.5
  339.8 3.8 copy-start.3
  343.7 17.1 %copy-start.15 = (bf16[512,1024]{1,0:T(8,128)(2,1)S(1)}, bf16[512,1024]{1,0:T(8,128)(2,1)}, u32[]{:S(2)}) copy-start(bf16[512,1024]{1,0:T(8,128)(2,1)} %all-gather.7.cloned.1.call-done) | copy-start | bytes 3145732
  358.4 26.0 %collective-permute-start.6 = (bf16[512,1024]{1,0:T(8,128)(2,1)}, bf16[512,1024]{1,0:T(8,128)(2,1)}, u32[]{:S(2)}, u32[]{:S(2)}) collective-permute-start(bf16[512,1024]{1,0:T(8,128)(2,1)} %all-gather.11.cloned.1.call-done), channel_id=1, source_target_pairs={{0,12},{4,8},{8,4},{12,0},{1,13},{5,9},{9,5},{13,1},{2,14},{6,10},... | collective-permute-start | bytes 3145736 | tf_op jit(solution)/shard_map/ppermute | solution.py:18
  362.2 1.0 copy-start.9
  362.2 3.9 copy-start.7
  366.0 18.3 %copy-start.17 = (bf16[512,1024]{1,0:T(8,128)(2,1)S(1)}, bf16[512,1024]{1,0:T(8,128)(2,1)}, u32[]{:S(2)}) copy-start(bf16[512,1024]{1,0:T(8,128)(2,1)} %all-gather.11.cloned.1.call-done) | copy-start | bytes 3145732
  385.7 1.0 copy-start.1
  405.7 83.4 %copy-start.18 = (bf16[1024,1024]{1,0:T(8,128)(2,1)S(1)}, bf16[1024,1024]{1,0:T(8,128)(2,1)}, u32[]{:S(2)}) copy-start(bf16[1024,1024]{1,0:T(8,128)(2,1)} %all-gather.5.cloned.1.call-done) | copy-start | bytes 6291460
  405.7 80.0 %collective-permute-start.8 = (bf16[1024,1792]{1,0:T(8,128)(2,1)S(1)}, bf16[1024,1792]{1,0:T(8,128)(2,1)S(1)}, u32[]{:S(2)}, u32[]{:S(2)}) collective-permute-start(bf16[1024,1792]{1,0:T(8,128)(2,1)S(1)} %get-tuple-element.11), channel_id=1, source_target_pairs={{0,8},{4,12},{8,0},{12,4},{1,9},{5,13},{9,1},{13,5},{2,10},{6,14},... | collective-permute-start | bytes 11010056 | tf_op jit(solution)/shard_map/ppermute | solution.py:18
  407.2 80.3 %collective-permute-start.7 = (bf16[1024,1792]{1,0:T(8,128)(2,1)S(1)}, bf16[1024,1792]{1,0:T(8,128)(2,1)S(1)}, u32[]{:S(2)}, u32[]{:S(2)}) collective-permute-start(bf16[1024,1792]{1,0:T(8,128)(2,1)S(1)} %get-tuple-element.11), channel_id=1, source_target_pairs={{0,4},{4,0},{8,12},{12,8},{1,5},{5,1},{9,13},{13,9},{2,6},{6,2},{1... | collective-permute-start | bytes 11010056 | tf_op jit(solution)/shard_map/ppermute | solution.py:18
  485.9 40.4 %collective-permute-start.10 = (bf16[512,1792]{1,0:T(8,128)(2,1)S(1)}, bf16[512,1792]{1,0:T(8,128)(2,1)S(1)}, u32[]{:S(2)}, u32[]{:S(2)}) collective-permute-start(bf16[512,1792]{1,0:T(8,128)(2,1)S(1)} %slice.31), channel_id=1, source_target_pairs={{0,4},{4,0},{8,12},{12,8},{1,5},{5,1},{9,13},{13,9},{2,6},{6,2},{1... | collective-permute-start | bytes 5505032 | tf_op jit(solution)/shard_map/ppermute | solution.py:18
  487.6 7.5 %copy-start.4 = (bf16[512,1024]{1,0:T(8,128)(2,1)S(1)}, bf16[512,1024]{1,0:T(8,128)(2,1)}, u32[]{:S(2)}) copy-start(bf16[512,1024]{1,0:T(8,128)(2,1)} %copy-done.3) | copy-start | bytes 3145732
  487.6 7.5 %copy-start.6 = (bf16[512,1024]{1,0:T(8,128)(2,1)S(1)}, bf16[512,1024]{1,0:T(8,128)(2,1)}, u32[]{:S(2)}) copy-start(bf16[512,1024]{1,0:T(8,128)(2,1)} %copy-done.5) | copy-start | bytes 3145732
  487.6 7.5 %copy-start.11 = (bf16[1024,1024]{0,1:T(8,128)(2,1)S(1)}, bf16[1024,1024]{0,1:T(8,128)(2,1)}, u32[]{:S(2)}) copy-start(bf16[1024,1024]{0,1:T(8,128)(2,1)} %copy.3) | copy-start | bytes 6291460
  487.6 39.6 %collective-permute-start.9 = (bf16[512,1792]{1,0:T(8,128)(2,1)S(1)}, bf16[512,1792]{1,0:T(8,128)(2,1)S(1)}, u32[]{:S(2)}, u32[]{:S(2)}) collective-permute-start(bf16[512,1792]{1,0:T(8,128)(2,1)S(1)} %slice.30), channel_id=1, source_target_pairs={{0,8},{4,12},{8,0},{12,4},{1,9},{5,13},{9,1},{13,5},{2,10},{6,14},... | collective-permute-start | bytes 5505032 | tf_op jit(solution)/shard_map/ppermute | solution.py:18
  495.1 7.1 %copy-start.8 = (bf16[512,1024]{1,0:T(8,128)(2,1)S(1)}, bf16[512,1024]{1,0:T(8,128)(2,1)}, u32[]{:S(2)}) copy-start(bf16[512,1024]{1,0:T(8,128)(2,1)} %copy-done.7) | copy-start | bytes 3145732
  495.1 7.0 %copy-start.10 = (bf16[512,1024]{1,0:T(8,128)(2,1)S(1)}, bf16[512,1024]{1,0:T(8,128)(2,1)}, u32[]{:S(2)}) copy-start(bf16[512,1024]{1,0:T(8,128)(2,1)} %copy-done.9) | copy-start | bytes 3145732
  495.1 7.0 %copy-start.12 = (bf16[1024,1024]{0,1:T(8,128)(2,1)S(1)}, bf16[1024,1024]{0,1:T(8,128)(2,1)}, u32[]{:S(2)}) copy-start(bf16[1024,1024]{0,1:T(8,128)(2,1)} %copy.2) | copy-start | bytes 6291460
  526.3 1.2 copy-start.13
  527.5 1.2 copy-start.14
Sparse Core Ops, SparseCore 0:
  95.5 28.6 reduce-scatter.8
  126.6 25.7 reduce-scatter.6
  154.7 42.4 reduce-scatter.4
  198.8 27.2 all-gather.8
  227.5 27.5 all-gather.6
  257.4 26.5 reduce-scatter.10
  285.5 44.5 all-gather.4
  331.7 26.6 all-gather.10

commit v3 on v2

--- a/solution.py
+++ b/solution.py
@@ -12,6 +12,8 @@
 quintic_first = 3.4445
 quintic_third = -4.775
 quintic_fifth = 2.0315
+
+PANELS = 2
 
 
 def swap(block, offset, count):
@@ -56,10 +58,21 @@
     eye = lax.broadcasted_iota(jnp.int32, (rows, rows), 0) == lax.broadcasted_iota(
         jnp.int32, (rows, rows), 1
     )
-    gram = [sum_over_columns(jnp.where(eye, 0.0, times_transpose(iterate, iterate)))]
+    own = jnp.where(eye, 0.0, times_transpose(iterate, iterate))
+    packed = sum_over_columns(jnp.concatenate([own[half:], own[:half, :half]], axis=1))
+    gram = [
+        jnp.concatenate(
+            [
+                jnp.concatenate([packed[:, rows:], packed[:, :half].T], axis=1),
+                packed[:, :rows],
+            ],
+            axis=0,
+        )
+    ]
+    arrived = [lax.optimization_barrier((packed, block))[1] for block in blocks[1:]]
     for offset in range(1, count):
         lower = (me & (1 << (offset.bit_length() - 1))) == 0
-        other = blocks[offset]
+        other = arrived[offset - 1]
         tall = jnp.where(lower, iterate, other)
         short = jnp.where(lower, other[:half], iterate[half:])
         mine = sum_over_columns(times_transpose(short, tall))
@@ -75,10 +88,17 @@
             total = total + jnp.dot(block, part, preferred_element_type=jnp.float32)
         return total
 
-    inner = quintic_third * wide + quintic_fifth * apply_gram(wide, blocks)
-    mixed = apply_gram(inner, gather_blocks(inner.astype(jnp.bfloat16), count))
     factor = 0.2 * math.sqrt(max(HEAD_FEATS, MODEL_DIM))
-    return (factor * (quintic_first * wide + mixed)).astype(jnp.bfloat16)
+    width = iterate.shape[1] // PANELS
+    updates = []
+    for p in range(PANELS):
+        columns = slice(p * width, (p + 1) * width)
+        own = wide[:, columns]
+        once = apply_gram(own, [block[:, columns] for block in blocks])
+        inner = quintic_third * own + quintic_fifth * once
+        mixed = apply_gram(inner, gather_blocks(inner.astype(jnp.bfloat16), count))
+        updates.append((factor * (quintic_first * own + mixed)).astype(jnp.bfloat16))
+    return jnp.concatenate(updates, axis=1)
 
 
 def solution(mesh):

time: 553 us -> 507 us (0.917)
  waiting for transfers between devices: 374 us -> 260 us
  local copies, waits for them, and re-layouts: 22.1 us -> 45.3 us
  other arithmetic: 7.8 us -> 28.4 us
  matrix products: 105 us -> 123 us
    ppermute x11 -> x15, waiting for transfers between devices: 198 us -> 132 us  [swap(): return lax.ppermute(block, 'row', [(i, i ^ offset) for i in range(count)])]
    reduce_scatter x4 -> x3, waiting for transfers between devices: 81.8 us -> 36.6 us  [sum_over_columns(): lax.psum_scatter(partial.astype(jnp.bfloat16), 'col', scatter_dimension=0...]
    all_gather x4, waiting for transfers between devices: 94 us -> 57.2 us  [sum_over_columns(): return lax.all_gather(owned, 'col', axis=0, tiled=True)]
    unnamed x8 -> x9, waiting for transfers between devices: 0.13 us -> 34.2 us
    dot_general x8 -> x16, matrix products: 80.9 us -> 100 us  [apply_gram(): total = total + jnp.dot(block, part, preferred_element_type=jnp.float32)]
    unnamed x39 -> x63, local copies, waits for them, and re-layouts: 6.5 us -> 15.6 us
    select_n x0 -> x3, other arithmetic: none -> 8.09 us  [shards(): gram.append(jnp.where(lower, pair.T, pair))]
    convert_element_type x0 -> x1, other arithmetic: none -> 5.96 us  [shards(): wide = iterate.astype(jnp.float32)]
  transfers between devices with their start and end apart: 19 -> 23, of which waited for: 15 -> 13; matrix products, arithmetic and copies ran while one was open for 17% -> 25% of each run, Pallas kernels for 0% -> 0%
where the time goes in v3:
time: 507 us; the launch traced here: 505 us
  waiting for transfers between devices  260 us (51%)
  matrix products  123 us (24%)
  local copies, waits for them, and re-layouts  45.3 us (9%)
  other arithmetic  28.4 us (6%)
  starting transfers between devices  23.7 us (5%)
  between operations  14 us (3%)
  blocking collectives  9.96 us (2%)
    ppermute x15, waiting for transfers between devices, swap(): return lax.ppermute(block, 'row', [(i, i ^ offset) for i in range(count)])  132 us
    dot_general x16, matrix products, apply_gram(): total = total + jnp.dot(block, part, preferred_element_type=jnp.float32)  100 us
    all_gather x4, waiting for transfers between devices, sum_over_columns(): return lax.all_gather(owned, 'col', axis=0, tiled=True)  57.2 us
    reduce_scatter x3, waiting for transfers between devices, sum_over_columns(): lax.psum_scatter(partial.astype(jnp.bfloat16), 'col', scatter_dimension=0...  36.6 us
    unnamed x9, waiting for transfers between devices  34.2 us
    ppermute x15, starting transfers between devices, swap(): return lax.ppermute(block, 'row', [(i, i ^ offset) for i in range(count)])  23.4 us
    dot_general x4, matrix products, times_transpose(): lax.dot_general(left, right, (((1,), (1,)), ((), ())), preferred_element_...  22.7 us
    unnamed x63, local copies, waits for them, and re-layouts  15.6 us
  transfers between devices with their start and end apart: 23, of which 13 were waited for; matrix products, arithmetic and copies ran while one was open for 25% of the time, Pallas kernels for 0%

profile of v3, /device:TPU:0, one launch (start us, length us, event | category | flops | bytes accessed | tf_op | source)
XLA Modules:
  0.0 504.6 jit_solution(14238999742820196635)
XLA Ops:
  6.5 7.1 %select_convert_fusion = bf16[1024,1024]{0,1:T(8,128)(2,1)S(1)} fusion(bf16[1024,1792]{1,0:T(8,128)(2,1)} %param.1), kind=kOutput, calls=%fused_computation.1 | convolution fusion | flops 3761242112 | bytes 5767168 | tf_op jit(solution)/shard_map/dot_general | solution.py:39
  13.9 1.6 copy.14
  15.6 3.0 collective-permute-start
  18.6 1.5 collective-permute-start.2
  20.1 33.6 %reduce-scatter.13.cloned.1.call-done = bf16[128,1536]{1,0:T(8,128)(2,1)} async-done(((bf16[512,1536]{1,0:T(8,128)(2,1)}), bf16[128,1536]{1,0:T(8,128)(2,1)}) %reduce-scatter.13.cloned.1.call-update) | async-done | bytes 393232
  53.7 1.9 copy.15
  55.7 42.6 %collective-permute-done = bf16[1024,1792]{1,0:T(8,128)(2,1)} collective-permute-done((bf16[1024,1792]{1,0:T(8,128)(2,1)}, bf16[1024,1792]{1,0:T(8,128)(2,1)}, u32[]{:S(2)}, u32[]{:S(2)}) %collective-permute-start) | collective-permute-done | bytes 3670048 | tf_op jit(solution)/shard_map/ppermute | solution.py:20
  98.2 2.8 slice.112
  101.1 1.8 collective-permute-start.4
  102.9 2.9 slice.113
  105.8 1.5 collective-permute-start.5
  107.3 6.3 %fusion.55 = bf16[512,1024]{1,0:T(8,128)(2,1)} fusion(bf16[1024,1792]{1,0:T(8,128)(2,1)} %param.1, bf16[1024,1792]{1,0:T(8,128)(2,1)} %collective-permute-done.2, pred[]{:T(512)S(6)} %eq.12), kind=kOutput, calls=%fused_computation.59 | convolution fusion | flops 1882324992 | bytes 12059648 | tf_op jit(solution)/shard_map/dot_general | solution.py:39
  113.6 28.9 %collective-permute-done.4 = bf16[512,1792]{1,0:T(8,128)(2,1)S(1)} collective-permute-done((bf16[512,1792]{1,0:T(8,128)(2,1)}, bf16[512,1792]{1,0:T(8,128)(2,1)S(1)}, u32[]{:S(2)}, u32[]{:S(2)}) %collective-permute-start.4) | collective-permute-done | bytes 1835040 | tf_op jit(solution)/shard_map/ppermute | solution.py:20
  142.6 4.1 collective-permute-done.5
  146.7 1.6 constant_dynamic-update-slice_fusion
  148.3 1.8 copy-done.4
  150.2 3.1 fusion.60
  153.3 6.2 %fusion.50 = bf16[512,1024]{1,0:T(8,128)(2,1)} fusion(bf16[1024,1792]{1,0:T(8,128)(2,1)} %param.1, bf16[1024,1792]{1,0:T(8,128)(2,1)} %collective-permute-done, pred[]{:T(512)S(6)} %eq.11), kind=kOutput, calls=%fused_computation.58 | convolution fusion | flops 1882324992 | bytes 12059648 | tf_op jit(solution)/shard_map/dot_general | solution.py:39
  160.2 20.6 %reduce-scatter.11.cloned.1.call-done = bf16[128,1024]{1,0:T(8,128)(2,1)} async-done(((bf16[512,1024]{1,0:T(8,128)(2,1)}), bf16[128,1024]{1,0:T(8,128)(2,1)}) %reduce-scatter.11.cloned.1.call-update) | async-done | bytes 262160 | tf_op jit(solution)/shard_map/reduce_scatter | solution.py:45
  180.9 6.0 %copy.8 = bf16[1024,1792]{0,1:T(8,128)(2,1)} copy(bf16[1024,1792]{1,0:T(8,128)(2,1)} %param.1) | data formatting | bytes 7340032 | tf_op args[0]
  186.9 6.0 %convert_element_type.25 = f32[1024,1792]{0,1:T(8,128)} convert(bf16[1024,1792]{0,1:T(8,128)(2,1)} %copy.8) | non-fusion elementwise | flops 1835008 | bytes 11010048 | tf_op jit(solution)/shard_map/convert_element_type | solution.py:54
  192.9 15.9 %reduce-scatter.7.cloned.1.call-done = bf16[128,1024]{1,0:T(8,128)(2,1)} async-done(((bf16[512,1024]{1,0:T(8,128)(2,1)}), bf16[128,1024]{1,0:T(8,128)(2,1)}) %reduce-scatter.7.cloned.1.call-update) | async-done | bytes 262160 | tf_op jit(solution)/shard_map/reduce_scatter | solution.py:45
  208.8 2.9 multiply_reduce_fusion
  211.7 10.0 %psum.7 = f32[1024]{0:T(1024)S(1)} all-reduce(f32[1024]{0:T(1024)S(1)} %multiply_reduce_fusion), channel_id=1, replica_groups=mesh['grp'=2,'row'=4,'col'=4] {'col'}, use_global_device_ids=true, to_apply=%region_1.0 | all-reduce | flops 1024 | bytes 8192 | tf_op jit(solution)/shard_map/psum | solution.py:57
  221.7 15.2 %all-gather.9.cloned.1.call-done = bf16[512,1024]{1,0:T(8,128)(2,1)} async-done(((bf16[128,1024]{1,0:T(8,128)(2,1)}), bf16[512,1024]{1,0:T(8,128)(2,1)}) %all-gather.9.cloned.1.call-update) | async-done | bytes 1048592 | tf_op jit(solution)/shard_map/all_gather | solution.py:46
  239.6 26.5 %all-gather.11.cloned.1.call-done = bf16[512,1024]{1,0:T(8,128)(2,1)} async-done(((bf16[128,1024]{1,0:T(8,128)(2,1)}), bf16[512,1024]{1,0:T(8,128)(2,1)}) %all-gather.11.cloned.1.call-update) | async-done | bytes 1048592 | tf_op jit(solution)/shard_map/all_gather | solution.py:46
  266.1 2.4 collective-permute-start.6
  268.5 5.7 %fusion.33 = f32[1024,896]{0,1:T(8,128)} fusion(bf16[1024,1792]{1,0:T(8,128)(2,1)} %param.1, bf16[512,1024]{0,1:T(8,128)(2,1)S(1)} %slice.109, bf16[512,512]{0,1:T(8,128)(2,1)S(1)} %bitcast.30, bf16[512,512]{0,1:T(8,128)(2,1)} %get-tuple-element.17), kind=kOutput, calls=%fused_computation.44 | convolution fusion | flops 1885339648 | bytes 7602176 | tf_op jit(solution)/shard_map/dot_general | solution.py:88
  274.2 5.5 %fusion.41 = f32[1024,896]{0,1:T(8,128)} fusion(bf16[1024,1792]{1,0:T(8,128)(2,1)S(1)} %copy-done.8, bf16[512,1024]{0,1:T(8,128)(2,1)} %copy-done.19, bf16[512,512]{0,1:T(8,128)(2,1)} %bitcast.31, bf16[512,512]{0,1:T(8,128)(2,1)S(1)} %copy-done.25), kind=kOutput, calls=%fused_computation.52 | convolution fusion | flops 1885339648 | bytes 7602176 | tf_op jit(solution)/shard_map/dot_general | solution.py:88
  279.7 15.5 %all-gather.7.cloned.1.call-done = bf16[512,1024]{1,0:T(8,128)(2,1)} async-done(((bf16[128,1024]{1,0:T(8,128)(2,1)}), bf16[512,1024]{1,0:T(8,128)(2,1)}) %all-gather.7.cloned.1.call-update) | async-done | bytes 1048592 | tf_op jit(solution)/shard_map/all_gather | solution.py:46
  298.1 1.5 pad_maximum_fusion.3
  299.6 3.9 copy.11
  303.5 1.7 broadcast_select_fusion.2
  306.2 1.7 fusion.68
  307.9 3.9 copy.12
  311.8 4.0 bitcast_select_fusion
  316.9 3.4 collective-permute-done.1
  322.6 1.7 pad_maximum_fusion.2
  324.3 3.9 copy.10
  328.2 3.0 bitcast_select_fusion.1
  331.3 6.3 %fusion.17 = f32[1024,896]{0,1:T(8,128)} fusion(bf16[1024,1024]{1,0:T(8,128)(2,1)S(1)} %copy-done.10, bf16[1024,1792]{1,0:T(8,128)(2,1)} %collective-permute-done.2), kind=kOutput, calls=%fused_computation.32 | convolution fusion | flops 1879048192 | bytes 7602176 | tf_op jit(solution)/shard_map/dot_general | solution.py:88
  337.7 5.7 %fusion.19 = f32[1024,896]{0,1:T(8,128)} fusion(bf16[1024,1024]{1,0:T(8,128)(2,1)S(1)} %bitcast_select_fusion.1, bf16[1024,1792]{1,0:T(8,128)(2,1)} %collective-permute-done), kind=kOutput, calls=%fused_computation.34 | convolution fusion | flops 1879048192 | bytes 7602176 | tf_op jit(solution)/shard_map/dot_general | solution.py:88
  343.4 18.3 %fusion.75 = (bf16[1024,896]{0,1:T(8,128)(2,1)}, f32[1024,896]{0,1:T(8,128)S(1)}) fusion(bf16[1024,1024]{1,0:T(8,128)(2,1)S(1)} %broadcast_select_fusion, bf16[1024,1792]{1,0:T(8,128)(2,1)S(1)} %copy-done.5, f32[1024,896]{0,1:T(8,128)} %fusion.17, f32[1024,896]{0,1:T(8,128)} %fusion.19, f32[1024,896]{0,1:T(8,128)S(1)} %copy-done.6, f32[1024]{0:T(1024)S(1)} %psum.7, ...), kind=kOutput, calls=%fused_computation.79 | convolution fusion | flops 1887305728 | bytes 24121344 | tf_op jit(solution)/shard_map/dot_general | solution.py:88
  361.7 1.5 collective-permute-start.8
  364.7 5.5 %fusion.11 = f32[1024,896]{0,1:T(8,128)} fusion(bf16[1024,1024]{1,0:T(8,128)(2,1)S(1)} %copy-done.10, bf16[1024,1792]{1,0:T(8,128)(2,1)} %collective-permute-done.2), kind=kOutput, calls=%fused_computation.26 | convolution fusion | flops 1879048192 | bytes 7602176 | tf_op jit(solution)/shard_map/dot_general | solution.py:88
  370.2 5.5 %fusion.13 = f32[1024,896]{0,1:T(8,128)} fusion(bf16[1024,1024]{1,0:T(8,128)(2,1)S(1)} %copy-done.13, bf16[1024,1792]{1,0:T(8,128)(2,1)} %collective-permute-done), kind=kOutput, calls=%fused_computation.28 | convolution fusion | flops 1879048192 | bytes 7602176 | tf_op jit(solution)/shard_map/dot_general | solution.py:88
  375.8 6.9 %fusion.74 = (bf16[1024,896]{0,1:T(8,128)(2,1)}, f32[1024,896]{0,1:T(8,128)S(1)}) fusion(bf16[1024,1024]{1,0:T(8,128)(2,1)S(1)} %broadcast_select_fusion, bf16[1024,1792]{1,0:T(8,128)(2,1)S(1)} %copy-done.5, f32[1024,896]{0,1:T(8,128)} %fusion.11, f32[1024,896]{0,1:T(8,128)} %fusion.13, f32[1024,896]{0,1:T(8,128)} %fusion.33, f32[1024]{0:T(1024)S(1)} %psum.7, ...), kind=kOutput, calls=%fused_computation.78 | convolution fusion | flops 1887305728 | bytes 24121344 | tf_op jit(solution)/shard_map/dot_general | solution.py:88
  383.8 5.0 fusion.71
  388.9 2.1 fusion.72
  390.9 14.1 %collective-permute-done.8 = bf16[1024,896]{0,1:T(8,128)(2,1)} collective-permute-done((bf16[1024,896]{0,1:T(8,128)(2,1)}, bf16[1024,896]{0,1:T(8,128)(2,1)}, u32[]{:S(2)}, u32[]{:S(2)}) %collective-permute-start.8) | collective-permute-done | bytes 1835040 | tf_op jit(solution)/shard_map/ppermute | solution.py:20
  406.3 1.5 collective-permute-start.10
  409.1 1.5 collective-permute-start.9
  410.6 33.6 %collective-permute-done.12 = bf16[1024,896]{0,1:T(8,128)(2,1)S(1)} collective-permute-done((bf16[1024,896]{0,1:T(8,128)(2,1)}, bf16[1024,896]{0,1:T(8,128)(2,1)S(1)}, u32[]{:S(2)}, u32[]{:S(2)}) %collective-permute-start.12) | collective-permute-done | bytes 1835040 | tf_op jit(solution)/shard_map/ppermute | solution.py:20
  444.4 1.5 collective-permute-start.14
  446.9 1.5 collective-permute-start.13
  448.4 5.5 %fusion.77 = f32[1024,896]{0,1:T(8,128)} fusion(bf16[1024,1024]{1,0:T(8,128)(2,1)S(1)} %copy-done.11, bf16[1024,896]{0,1:T(8,128)(2,1)} %collective-permute-done.8), kind=kOutput, calls=%fused_computation.81 | convolution fusion | flops 1879048192 | bytes 7602176 | tf_op jit(solution)/shard_map/dot_general | solution.py:88
  453.9 5.5 %fusion.76 = f32[1024,896]{0,1:T(8,128)} fusion(bf16[1024,1024]{1,0:T(8,128)(2,1)S(1)} %copy-done.14, bf16[1024,896]{0,1:T(8,128)(2,1)} %collective-permute-done.7), kind=kOutput, calls=%fused_computation.80 | convolution fusion | flops 1879048192 | bytes 7602176 | tf_op jit(solution)/shard_map/dot_general | solution.py:88
  459.5 3.9 fusion.79
  463.4 3.9 fusion.78
  469.2 8.0 %multiply_convert_fusion.1 = bf16[1024,896]{0,1:T(8,128)(2,1)S(1)} fusion(f32[1024,896]{0,1:T(8,128)} %fusion.77, f32[1024,896]{0,1:T(8,128)} %fusion.76, f32[1024,896]{0,1:T(8,128)} %fusion.71, f32[1024,896]{0,1:T(8,128)S(1)} %get-tuple-element.22, f32[1024,1792]{0,1:T(8,128)S(1)} %bitcast.29, bf16[1024,1024]{1,0:T(8,128)(2,1)S(1)} %broadcast_select_fusion, ...), kind=kOutput, calls=%fused_computation.6 | convolution fusion | flops 1890975744 | bytes 24121344 | tf_op jit(solution)/shard_map/dot_general | solution.py:88
  477.1 5.5 %collective-permute-done.14 = bf16[512,896]{0,1:T(8,128)(2,1)} collective-permute-done((bf16[512,896]{0,1:T(8,128)(2,1)S(1)}, bf16[512,896]{0,1:T(8,128)(2,1)}, u32[]{:S(2)}, u32[]{:S(2)}) %collective-permute-start.14) | collective-permute-done | bytes 917536 | tf_op jit(solution)/shard_map/ppermute | solution.py:20
  482.7 6.8 %multiply_convert_fusion = bf16[1024,896]{0,1:T(8,128)(2,1)S(1)} fusion(f32[1024,896]{0,1:T(8,128)} %fusion.79, f32[1024,896]{0,1:T(8,128)} %fusion.78, f32[1024,896]{0,1:T(8,128)S(1)} %fusion.72, f32[1024,896]{0,1:T(8,128)S(1)} %get-tuple-element.20, f32[1024,1792]{0,1:T(8,128)S(1)} %bitcast.29, bf16[1024,1024]{1,0:T(8,128)(2,1)S(1)} %broadcast_select_fusion, ...), kind=kOutput, calls=%fused_computation.4 | convolution fusion | flops 1890975744 | bytes 24121344 | tf_op jit(solution)/shard_map/dot_general | solution.py:88
  489.5 2.2 pad_maximum_fusion
  491.6 5.9 %copy.13 = bf16[1024,1792]{1,0:T(8,128)(2,1)} copy(bf16[1024,1792]{0,1:T(8,128)(2,1)} %pad_maximum_fusion) | data formatting | bytes 7340032 | tf_op jit(solution)/shard_map/concatenate | solution.py:101
  (103 shorter events, 19.3 us)
Async XLA Ops:
  6.5 47.2 %reduce-scatter.13.cloned.1.call-start = ((), (), s32[]{:S(2)}) async-start(), calls=%async_computation.11 | async-start | bytes 1966080
  15.5 91.7 %all-gather.5.cloned.1.call-start = ((), (), s32[]{:S(2)}) async-start(), calls=%async_computation.4 | async-start | bytes 1966080 | tf_op jit(solution)/shard_map/all_gather | solution.py:46
  15.6 82.7 %collective-permute-start = (bf16[1024,1792]{1,0:T(8,128)(2,1)}, bf16[1024,1792]{1,0:T(8,128)(2,1)}, u32[]{:S(2)}, u32[]{:S(2)}) collective-permute-start(bf16[1024,1792]{1,0:T(8,128)(2,1)} %param.1), channel_id=1, source_target_pairs={{0,4},{4,0},{8,12},{12,8},{1,5},{5,1},{9,13},{13,9},{2,6},{6,2},{1... | collective-permute-start | bytes 11010056 | tf_op jit(solution)/shard_map/ppermute | solution.py:20
  18.6 84.3 %collective-permute-start.2 = (bf16[1024,1792]{1,0:T(8,128)(2,1)}, bf16[1024,1792]{1,0:T(8,128)(2,1)}, u32[]{:S(2)}, u32[]{:S(2)}) collective-permute-start(bf16[1024,1792]{1,0:T(8,128)(2,1)} %param.1), channel_id=1, source_target_pairs={{0,8},{4,12},{8,0},{12,4},{1,9},{5,13},{9,1},{13,5},{2,10},{6,14},... | collective-permute-start | bytes 11010056 | tf_op jit(solution)/shard_map/ppermute | solution.py:20
  55.6 104.0 %reduce-scatter.9.cloned.1.call-start = ((), (), s32[]{:S(2)}) async-start(), calls=%async_computation.7 | async-start | bytes 1310720 | tf_op jit(solution)/shard_map/reduce_scatter | solution.py:45
  101.1 41.4 %collective-permute-start.4 = (bf16[512,1792]{1,0:T(8,128)(2,1)}, bf16[512,1792]{1,0:T(8,128)(2,1)S(1)}, u32[]{:S(2)}, u32[]{:S(2)}) collective-permute-start(bf16[512,1792]{1,0:T(8,128)(2,1)} %slice.112), channel_id=1, source_target_pairs={{0,8},{4,12},{8,0},{12,4},{1,9},{5,13},{9,1},{13,5},{2,10},{6,14},... | collective-permute-start | bytes 5505032 | tf_op jit(solution)/shard_map/ppermute | solution.py:20
  105.8 40.9 %collective-permute-start.5 = (bf16[512,1792]{1,0:T(8,128)(2,1)}, bf16[512,1792]{1,0:T(8,128)(2,1)}, u32[]{:S(2)}, u32[]{:S(2)}) collective-permute-start(bf16[512,1792]{1,0:T(8,128)(2,1)} %slice.113), channel_id=1, source_target_pairs={{0,4},{4,0},{8,12},{12,8},{1,5},{5,1},{9,13},{13,9},{2,6},{6,2},{1... | collective-permute-start | bytes 5505032 | tf_op jit(solution)/shard_map/ppermute | solution.py:20
  113.5 67.3 %reduce-scatter.11.cloned.1.call-start = ((), (), s32[]{:S(2)}) async-start(), calls=%async_computation.9 | async-start | bytes 1310720 | tf_op jit(solution)/shard_map/reduce_scatter | solution.py:45
  113.6 36.6 %copy-start.7 = (bf16[1024,1792]{1,0:T(8,128)(2,1)S(1)}, bf16[1024,1792]{1,0:T(8,128)(2,1)}, u32[]{:S(2)}) copy-start(bf16[1024,1792]{1,0:T(8,128)(2,1)} %param.1) | copy-start | bytes 11010052
  148.3 1.8 copy-start.4
  153.3 55.5 %reduce-scatter.7.cloned.1.call-start = ((), (), s32[]{:S(2)}) async-start(), calls=%async_computation.5 | async-start | bytes 1310720 | tf_op jit(solution)/shard_map/reduce_scatter | solution.py:45
  159.6 77.4 %all-gather.9.cloned.1.call-start = ((), (), s32[]{:S(2)}) async-start(), calls=%async_computation.8 | async-start | bytes 1310720 | tf_op jit(solution)/shard_map/all_gather | solution.py:46
  160.2 105.9 %all-gather.11.cloned.1.call-start = ((), (), s32[]{:S(2)}) async-start(), calls=%async_computation.10 | async-start | bytes 1310720 | tf_op jit(solution)/shard_map/all_gather | solution.py:46
  180.9 114.3 %all-gather.7.cloned.1.call-start = ((), (), s32[]{:S(2)}) async-start(), calls=%async_computation.6 | async-start | bytes 1310720 | tf_op jit(solution)/shard_map/all_gather | solution.py:46
  192.9 45.6 %copy-start.9 = (bf16[512,1536]{0,1:T(8,128)(2,1)S(1)}, bf16[512,1536]{0,1:T(8,128)(2,1)}, u32[]{:S(2)}) copy-start(bf16[512,1536]{0,1:T(8,128)(2,1)} %all-gather.5.cloned.1.call-done) | copy-start | bytes 4718596
  237.0 59.7 %collective-permute-start.3 = (bf16[512,1024]{1,0:T(8,128)(2,1)}, bf16[512,1024]{1,0:T(8,128)(2,1)}, u32[]{:S(2)}, u32[]{:S(2)}) collective-permute-start(bf16[512,1024]{1,0:T(8,128)(2,1)} %all-gather.9.cloned.1.call-done), channel_id=1, source_target_pairs={{0,8},{4,12},{8,0},{12,4},{1,9},{5,13},{9,1},{13,5},{2,10},{6,14},... | collective-permute-start | bytes 3145736 | tf_op jit(solution)/shard_map/ppermute | solution.py:20
  239.5 28.9 %copy-start.23 = (bf16[512,512]{1,0:T(8,128)(2,1)}, bf16[512,512]{1,0:T(8,128)(2,1)S(1)}, u32[]{:S(2)}) copy-start(bf16[512,512]{1,0:T(8,128)(2,1)S(1)} %copy.16) | copy-start | bytes 1572868
  239.6 28.9 %copy-start.19 = (bf16[512,1024]{0,1:T(8,128)(2,1)}, bf16[512,1024]{0,1:T(8,128)(2,1)S(1)}, u32[]{:S(2)}) copy-start(bf16[512,1024]{0,1:T(8,128)(2,1)S(1)} %slice.109) | copy-start | bytes 3145732
  266.1 37.4 %collective-permute-start.6 = (bf16[512,1024]{1,0:T(8,128)(2,1)}, bf16[512,1024]{1,0:T(8,128)(2,1)}, u32[]{:S(2)}, u32[]{:S(2)}) collective-permute-start(bf16[512,1024]{1,0:T(8,128)(2,1)} %all-gather.11.cloned.1.call-done), channel_id=1, source_target_pairs={{0,12},{4,8},{8,4},{12,0},{1,13},{5,9},{9,5},{13,1},{2,14},{6,10},... | collective-permute-start | bytes 3145736 | tf_op jit(solution)/shard_map/ppermute | solution.py:20
  268.5 5.7 %copy-start.8 = (bf16[1024,1792]{1,0:T(8,128)(2,1)S(1)}, bf16[1024,1792]{1,0:T(8,128)(2,1)}, u32[]{:S(2)}) copy-start(bf16[1024,1792]{1,0:T(8,128)(2,1)} %param.1) | copy-start | bytes 11010052
  268.5 5.7 %copy-start.25 = (bf16[512,512]{0,1:T(8,128)(2,1)S(1)}, bf16[512,512]{0,1:T(8,128)(2,1)}, u32[]{:S(2)}) copy-start(bf16[512,512]{0,1:T(8,128)(2,1)} %get-tuple-element.17) | copy-start | bytes 1572868
  274.2 22.5 %copy-start.18 = (bf16[512,1024]{1,0:T(8,128)(2,1)S(1)}, bf16[512,1024]{1,0:T(8,128)(2,1)}, u32[]{:S(2)}) copy-start(bf16[512,1024]{1,0:T(8,128)(2,1)} %all-gather.9.cloned.1.call-done) | copy-start | bytes 3145732
  295.2 25.1 %collective-permute-start.1 = (bf16[512,1024]{1,0:T(8,128)(2,1)}, bf16[512,1024]{1,0:T(8,128)(2,1)}, u32[]{:S(2)}, u32[]{:S(2)}) collective-permute-start(bf16[512,1024]{1,0:T(8,128)(2,1)} %all-gather.7.cloned.1.call-done), channel_id=1, source_target_pairs={{0,4},{4,0},{8,12},{12,8},{1,5},{5,1},{9,13},{13,9},{2,6},{6,2},{1... | collective-permute-start | bytes 3145736 | tf_op jit(solution)/shard_map/ppermute | solution.py:20
  305.2 1.0 copy-start
  311.8 4.1 copy-start.1
  311.8 4.1 copy-start.3
  315.9 4.4 copy-start.17
  321.7 1.0 copy-start.2
  328.2 3.1 copy-start.10
  328.2 15.1 %slice-start = ((s8[7340032]{0:T(1024)(128)(4,1)}), s8[4194304]{0:T(1024)(128)(4,1)S(1)}, s32[]{:S(2)}) async-start(s8[7340032]{0:T(1024)(128)(4,1)} %bitcast.28), calls=%async_computation.12 | async-start | bytes 8388608
  331.3 6.4 %copy-start.12 = (bf16[1024,1024]{1,0:T(8,128)(2,1)}, bf16[1024,1024]{1,0:T(8,128)(2,1)S(1)}, u32[]{:S(2)}) copy-start(bf16[1024,1024]{1,0:T(8,128)(2,1)S(1)} %bitcast_select_fusion.1) | copy-start | bytes 6291460
  331.3 12.1 %slice-start.1 = ((s8[7340032]{0:T(1024)(128)(4,1)}), s8[3145728]{0:T(1024)(128)(4,1)S(1)}, s32[]{:S(2)}) async-start(s8[7340032]{0:T(1024)(128)(4,1)} %bitcast.28), calls=%async_computation.13 | async-start | bytes 6291456
  337.6 5.7 %copy-start.5 = (bf16[1024,1792]{1,0:T(8,128)(2,1)S(1)}, bf16[1024,1792]{1,0:T(8,128)(2,1)}, u32[]{:S(2)}) copy-start(bf16[1024,1792]{1,0:T(8,128)(2,1)} %copy-done.4) | copy-start | bytes 11010052
  337.7 5.7 %copy-start.6 = (f32[1024,896]{0,1:T(8,128)S(1)}, f32[1024,896]{0,1:T(8,128)}, u32[]{:S(2)}) copy-start(f32[1024,896]{0,1:T(8,128)} %fusion.41) | copy-start | bytes 11010052
  361.7 8.5 %copy-start.13 = (bf16[1024,1024]{1,0:T(8,128)(2,1)S(1)}, bf16[1024,1024]{1,0:T(8,128)(2,1)}, u32[]{:S(2)}) copy-start(bf16[1024,1024]{1,0:T(8,128)(2,1)} %copy-done.12) | copy-start | bytes 6291460
  361.7 43.3 %collective-permute-start.8 = (bf16[1024,896]{0,1:T(8,128)(2,1)}, bf16[1024,896]{0,1:T(8,128)(2,1)}, u32[]{:S(2)}, u32[]{:S(2)}) collective-permute-start(bf16[1024,896]{0,1:T(8,128)(2,1)} %get-tuple-element.21), channel_id=1, source_target_pairs={{0,8},{4,12},{8,0},{12,4},{1,9},{5,13},{9,1},{13,5},{2,10},{6,14},... | collective-permute-start | bytes 5505032 | tf_op jit(solution)/shard_map/ppermute | solution.py:20
  363.3 44.6 %collective-permute-start.7 = (bf16[1024,896]{0,1:T(8,128)(2,1)}, bf16[1024,896]{0,1:T(8,128)(2,1)}, u32[]{:S(2)}, u32[]{:S(2)}) collective-permute-start(bf16[1024,896]{0,1:T(8,128)(2,1)} %get-tuple-element.21), channel_id=1, source_target_pairs={{0,4},{4,0},{8,12},{12,8},{1,5},{5,1},{9,13},{13,9},{2,6},{6,2},{1... | collective-permute-start | bytes 5505032 | tf_op jit(solution)/shard_map/ppermute | solution.py:20
  375.7 8.0 %copy-start.15 = (bf16[1024,896]{0,1:T(8,128)(2,1)S(1)}, bf16[1024,896]{0,1:T(8,128)(2,1)}, u32[]{:S(2)}) copy-start(bf16[1024,896]{0,1:T(8,128)(2,1)} %get-tuple-element.21) | copy-start | bytes 5505028
  375.8 8.0 %copy-start.20 = (bf16[512,1024]{0,1:T(8,128)(2,1)S(1)}, bf16[512,1024]{0,1:T(8,128)(2,1)}, u32[]{:S(2)}) copy-start(bf16[512,1024]{0,1:T(8,128)(2,1)} %copy-done.19) | copy-start | bytes 3145732
  382.6 6.2 %copy-start.16 = (bf16[1024,896]{0,1:T(8,128)(2,1)S(1)}, bf16[1024,896]{0,1:T(8,128)(2,1)}, u32[]{:S(2)}) copy-start(bf16[1024,896]{0,1:T(8,128)(2,1)} %get-tuple-element.19) | copy-start | bytes 5505028
  382.6 6.2 %copy-start.24 = (bf16[512,512]{1,0:T(8,128)(2,1)S(1)}, bf16[512,512]{1,0:T(8,128)(2,1)}, u32[]{:S(2)}) copy-start(bf16[512,512]{1,0:T(8,128)(2,1)} %copy-done.23) | copy-start | bytes 1572868
  382.6 6.2 %copy-start.26 = (bf16[512,512]{0,1:T(8,128)(2,1)S(1)}, bf16[512,512]{0,1:T(8,128)(2,1)}, u32[]{:S(2)}) copy-start(bf16[512,512]{0,1:T(8,128)(2,1)} %get-tuple-element.17) | copy-start | bytes 1572868
  382.6 61.6 %collective-permute-start.12 = (bf16[1024,896]{0,1:T(8,128)(2,1)}, bf16[1024,896]{0,1:T(8,128)(2,1)S(1)}, u32[]{:S(2)}, u32[]{:S(2)}) collective-permute-start(bf16[1024,896]{0,1:T(8,128)(2,1)} %get-tuple-element.19), channel_id=1, source_target_pairs={{0,8},{4,12},{8,0},{12,4},{1,9},{5,13},{9,1},{13,5},{2,10},{6,14},... | collective-permute-start | bytes 5505032 | tf_op jit(solution)/shard_map/ppermute | solution.py:20
  383.2 62.6 %collective-permute-start.11 = (bf16[1024,896]{0,1:T(8,128)(2,1)}, bf16[1024,896]{0,1:T(8,128)(2,1)S(1)}, u32[]{:S(2)}, u32[]{:S(2)}) collective-permute-start(bf16[1024,896]{0,1:T(8,128)(2,1)} %get-tuple-element.19), channel_id=1, source_target_pairs={{0,4},{4,0},{8,12},{12,8},{1,5},{5,1},{9,13},{13,9},{2,6},{6,2},{1... | collective-permute-start | bytes 5505032 | tf_op jit(solution)/shard_map/ppermute | solution.py:20
  390.9 57.5 %copy-start.11 = (bf16[1024,1024]{1,0:T(8,128)(2,1)S(1)}, bf16[1024,1024]{1,0:T(8,128)(2,1)}, u32[]{:S(2)}) copy-start(bf16[1024,1024]{1,0:T(8,128)(2,1)} %bitcast_select_fusion) | copy-start | bytes 6291460
  406.3 61.0 %collective-permute-start.10 = (bf16[512,896]{0,1:T(8,128)(2,1)S(1)}, bf16[512,896]{0,1:T(8,128)(2,1)S(1)}, u32[]{:S(2)}, u32[]{:S(2)}) collective-permute-start(bf16[512,896]{0,1:T(8,128)(2,1)S(1)} %slice.116), channel_id=1, source_target_pairs={{0,4},{4,0},{8,12},{12,8},{1,5},{5,1},{9,13},{13,9},{2,6},{6,2},{1... | collective-permute-start | bytes 2752520 | tf_op jit(solution)/shard_map/ppermute | solution.py:20
  409.1 58.2 %collective-permute-start.9 = (bf16[512,896]{0,1:T(8,128)(2,1)S(1)}, bf16[512,896]{0,1:T(8,128)(2,1)S(1)}, u32[]{:S(2)}, u32[]{:S(2)}) collective-permute-start(bf16[512,896]{0,1:T(8,128)(2,1)S(1)} %slice.115), channel_id=1, source_target_pairs={{0,8},{4,12},{8,0},{12,4},{1,9},{5,13},{9,1},{13,5},{2,10},{6,14},... | collective-permute-start | bytes 2752520 | tf_op jit(solution)/shard_map/ppermute | solution.py:20
  444.4 38.3 %collective-permute-start.14 = (bf16[512,896]{0,1:T(8,128)(2,1)S(1)}, bf16[512,896]{0,1:T(8,128)(2,1)}, u32[]{:S(2)}, u32[]{:S(2)}) collective-permute-start(bf16[512,896]{0,1:T(8,128)(2,1)S(1)} %slice.122), channel_id=1, source_target_pairs={{0,4},{4,0},{8,12},{12,8},{1,5},{5,1},{9,13},{13,9},{2,6},{6,2},{1... | collective-permute-start | bytes 2752520 | tf_op jit(solution)/shard_map/ppermute | solution.py:20
  446.9 7.0 %copy-start.14 = (bf16[1024,1024]{1,0:T(8,128)(2,1)S(1)}, bf16[1024,1024]{1,0:T(8,128)(2,1)}, u32[]{:S(2)}) copy-start(bf16[1024,1024]{1,0:T(8,128)(2,1)} %copy-done.12) | copy-start | bytes 6291460
  446.9 35.7 %collective-permute-start.13 = (bf16[512,896]{0,1:T(8,128)(2,1)}, bf16[512,896]{0,1:T(8,128)(2,1)}, u32[]{:S(2)}, u32[]{:S(2)}) collective-permute-start(bf16[512,896]{0,1:T(8,128)(2,1)} %slice.121), channel_id=1, source_target_pairs={{0,8},{4,12},{8,0},{12,4},{1,9},{5,13},{9,1},{13,5},{2,10},{6,14},... | collective-permute-start | bytes 2752520 | tf_op jit(solution)/shard_map/ppermute | solution.py:20
  467.3 0.9 copy-start.21
  468.2 0.9 copy-start.22
Sparse Core Ops, SparseCore 0:
  15.7 37.9 reduce-scatter.12
  55.8 36.6 all-gather.4
  113.7 26.4 reduce-scatter.8
  153.4 27.4 reduce-scatter.10
  183.0 25.7 reduce-scatter.6
  210.3 26.5 all-gather.8
  238.6 27.4 all-gather.10
  267.8 27.4 all-gather.6

commit v4 on v3

--- a/solution.py
+++ b/solution.py
@@ -69,13 +69,14 @@
             axis=0,
         )
     ]
-    arrived = [lax.optimization_barrier((packed, block))[1] for block in blocks[1:]]
+    before = packed
     for offset in range(1, count):
         lower = (me & (1 << (offset.bit_length() - 1))) == 0
-        other = arrived[offset - 1]
+        before, other = lax.optimization_barrier((before, blocks[offset]))
         tall = jnp.where(lower, iterate, other)
         short = jnp.where(lower, other[:half], iterate[half:])
-        mine = sum_over_columns(times_transpose(short, tall))
+        before = times_transpose(short, tall).astype(jnp.bfloat16)
+        mine = sum_over_columns(before)
         theirs = swap(mine, offset, count)
         pair = jnp.concatenate(
             [jnp.where(lower, mine, theirs), jnp.where(lower, theirs, mine)], axis=0

time: 507 us -> 541 us (1.067)
  waiting for transfers between devices: 260 us -> 298 us
    reduce_scatter x3, waiting for transfers between devices: 36.6 us -> 73.5 us  [sum_over_columns(): lax.psum_scatter(partial.astype(jnp.bfloat16), 'col', scatter_dimension=0...]
    unnamed x63 -> x67, local copies, waits for them, and re-layouts: 15.6 us -> 16.5 us
  transfers between devices with their start and end apart: 23 -> 23, of which waited for: 13 -> 13; matrix products, arithmetic and copies ran while one was open for 25% -> 21% of each run, Pallas kernels for 0% -> 0%
where the time goes in v4:
time: 541 us; the launch traced here: 539 us
  waiting for transfers between devices  298 us (55%)
  matrix products  122 us (23%)
  local copies, waits for them, and re-layouts  44.9 us (8%)
  other arithmetic  26 us (5%)
  starting transfers between devices  23.6 us (4%)
  between operations  14 us (3%)
  blocking collectives  9.94 us (2%)
    ppermute x15, waiting for transfers between devices, swap(): return lax.ppermute(block, 'row', [(i, i ^ offset) for i in range(count)])  131 us
    dot_general x16, matrix products, apply_gram(): total = total + jnp.dot(block, part, preferred_element_type=jnp.float32)  99.4 us
    reduce_scatter x3, waiting for transfers between devices, sum_over_columns(): lax.psum_scatter(partial.astype(jnp.bfloat16), 'col', scatter_dimension=0...  73.5 us
    all_gather x4, waiting for transfers between devices, sum_over_columns(): return lax.all_gather(owned, 'col', axis=0, tiled=True)  58.7 us
    unnamed x9, waiting for transfers between devices  34.7 us
    ppermute x15, starting transfers between devices, swap(): return lax.ppermute(block, 'row', [(i, i ^ offset) for i in range(count)])  23.3 us
    dot_general x4, matrix products, times_transpose(): lax.dot_general(left, right, (((1,), (1,)), ((), ())), preferred_element_...  22.7 us
    unnamed x67, local copies, waits for them, and re-layouts  16.5 us
  transfers between devices with their start and end apart: 23, of which 13 were waited for; matrix products, arithmetic and copies ran while one was open for 21% of the time, Pallas kernels for 0%

profile of v4, /device:TPU:0, one launch (start us, length us, event | category | flops | bytes accessed | tf_op | source)
XLA Modules:
  0.0 538.8 jit_solution(3055873846631873369)
XLA Ops:
  6.5 7.1 %select_convert_fusion = bf16[1024,1024]{0,1:T(8,128)(2,1)S(1)} fusion(bf16[1024,1792]{1,0:T(8,128)(2,1)} %param.1), kind=kOutput, calls=%fused_computation.1 | convolution fusion | flops 3761242112 | bytes 5767168 | tf_op jit(solution)/shard_map/dot_general | solution.py:39
  13.9 1.6 copy.14
  15.6 3.0 collective-permute-start
  18.6 1.5 collective-permute-start.2
  20.1 33.6 %reduce-scatter.13.cloned.1.call-done = bf16[128,1536]{1,0:T(8,128)(2,1)} async-done(((bf16[512,1536]{1,0:T(8,128)(2,1)}), bf16[128,1536]{1,0:T(8,128)(2,1)}) %reduce-scatter.13.cloned.1.call-update) | async-done | bytes 393232
  53.7 1.9 copy.15
  55.7 42.5 %collective-permute-done = bf16[1024,1792]{1,0:T(8,128)(2,1)} collective-permute-done((bf16[1024,1792]{1,0:T(8,128)(2,1)}, bf16[1024,1792]{1,0:T(8,128)(2,1)}, u32[]{:S(2)}, u32[]{:S(2)}) %collective-permute-start) | collective-permute-done | bytes 3670048 | tf_op jit(solution)/shard_map/ppermute | solution.py:20
  98.2 2.8 slice.112
  101.1 1.8 collective-permute-start.4
  102.9 2.9 slice.113
  105.8 1.5 collective-permute-start.5
  107.2 6.3 %fusion.50 = bf16[512,1024]{1,0:T(8,128)(2,1)} fusion(bf16[1024,1792]{1,0:T(8,128)(2,1)} %param.1, bf16[1024,1792]{1,0:T(8,128)(2,1)} %collective-permute-done, pred[]{:T(512)S(6)} %eq.11), kind=kOutput, calls=%fused_computation.58 | convolution fusion | flops 1882324992 | bytes 12059648 | tf_op jit(solution)/shard_map/dot_general | solution.py:39
  113.5 29.0 %collective-permute-done.4 = bf16[512,1792]{1,0:T(8,128)(2,1)S(1)} collective-permute-done((bf16[512,1792]{1,0:T(8,128)(2,1)}, bf16[512,1792]{1,0:T(8,128)(2,1)S(1)}, u32[]{:S(2)}, u32[]{:S(2)}) %collective-permute-start.4) | collective-permute-done | bytes 1835040 | tf_op jit(solution)/shard_map/ppermute | solution.py:20
  143.8 4.6 fusion.55
  148.5 3.0 constant_dynamic-update-slice_fusion
  151.5 4.7 fusion.60
  157.4 29.6 %reduce-scatter.11.cloned.1.call-done = bf16[128,1024]{1,0:T(8,128)(2,1)} async-done(((bf16[512,1024]{1,0:T(8,128)(2,1)}), bf16[128,1024]{1,0:T(8,128)(2,1)}) %reduce-scatter.11.cloned.1.call-update) | async-done | bytes 262160 | tf_op jit(solution)/shard_map/reduce_scatter | solution.py:45
  187.0 28.0 %reduce-scatter.7.cloned.1.call-done = bf16[128,1024]{1,0:T(8,128)(2,1)} async-done(((bf16[512,1024]{1,0:T(8,128)(2,1)}), bf16[128,1024]{1,0:T(8,128)(2,1)}) %reduce-scatter.7.cloned.1.call-update) | async-done | bytes 262160 | tf_op jit(solution)/shard_map/reduce_scatter | solution.py:45
  215.1 5.9 %copy.8 = bf16[1024,1792]{0,1:T(8,128)(2,1)} copy(bf16[1024,1792]{1,0:T(8,128)(2,1)} %param.1) | data formatting | bytes 7340032 | tf_op args[0]
  221.0 6.0 %convert_element_type.25 = f32[1024,1792]{0,1:T(8,128)} convert(bf16[1024,1792]{0,1:T(8,128)(2,1)} %copy.8) | non-fusion elementwise | flops 1835008 | bytes 11010048 | tf_op jit(solution)/shard_map/convert_element_type | solution.py:54
  227.0 16.0 %reduce-scatter.9.cloned.1.call-done = bf16[128,1024]{1,0:T(8,128)(2,1)} async-done(((bf16[512,1024]{1,0:T(8,128)(2,1)}), bf16[128,1024]{1,0:T(8,128)(2,1)}) %reduce-scatter.9.cloned.1.call-update) | async-done | bytes 262160 | tf_op jit(solution)/shard_map/reduce_scatter | solution.py:45
  243.0 2.9 multiply_reduce_fusion
  245.9 9.9 %psum.7 = f32[1024]{0:T(1024)S(1)} all-reduce(f32[1024]{0:T(1024)S(1)} %multiply_reduce_fusion), channel_id=1, replica_groups=mesh['grp'=2,'row'=4,'col'=4] {'col'}, use_global_device_ids=true, to_apply=%region_1.0 | all-reduce | flops 1024 | bytes 8192 | tf_op jit(solution)/shard_map/psum | solution.py:57
  255.9 15.3 %all-gather.11.cloned.1.call-done = bf16[512,1024]{1,0:T(8,128)(2,1)} async-done(((bf16[128,1024]{1,0:T(8,128)(2,1)}), bf16[512,1024]{1,0:T(8,128)(2,1)}) %all-gather.11.cloned.1.call-update) | async-done | bytes 1048592 | tf_op jit(solution)/shard_map/all_gather | solution.py:46
  271.2 2.3 collective-permute-start.6
  274.7 25.6 %all-gather.7.cloned.1.call-done = bf16[512,1024]{1,0:T(8,128)(2,1)} async-done(((bf16[128,1024]{1,0:T(8,128)(2,1)}), bf16[512,1024]{1,0:T(8,128)(2,1)}) %all-gather.7.cloned.1.call-update) | async-done | bytes 1048592 | tf_op jit(solution)/shard_map/all_gather | solution.py:46
  301.7 5.7 %fusion.33 = f32[1024,896]{0,1:T(8,128)} fusion(bf16[1024,1792]{1,0:T(8,128)(2,1)} %param.1, bf16[512,1024]{0,1:T(8,128)(2,1)S(1)} %slice.109, bf16[512,512]{0,1:T(8,128)(2,1)S(1)} %bitcast.30, bf16[512,512]{0,1:T(8,128)(2,1)} %get-tuple-element.17), kind=kOutput, calls=%fused_computation.44 | convolution fusion | flops 1885339648 | bytes 7602176 | tf_op jit(solution)/shard_map/dot_general | solution.py:89
  307.5 4.0 fusion.41
  311.5 17.9 %all-gather.9.cloned.1.call-done = bf16[512,1024]{1,0:T(8,128)(2,1)} async-done(((bf16[128,1024]{1,0:T(8,128)(2,1)}), bf16[512,1024]{1,0:T(8,128)(2,1)}) %all-gather.9.cloned.1.call-update) | async-done | bytes 1048592 | tf_op jit(solution)/shard_map/all_gather | solution.py:46
  329.4 1.5 collective-permute-start.3
  333.5 2.6 copy.12
  336.0 1.7 broadcast_select_fusion.6
  339.3 2.6 copy.10
  342.0 3.0 broadcast_select_fusion
  345.1 2.3 bitcast_select_fusion.1
  347.4 7.0 %collective-permute-done.3 = bf16[512,1024]{1,0:T(8,128)(2,1)} collective-permute-done((bf16[512,1024]{1,0:T(8,128)(2,1)}, bf16[512,1024]{1,0:T(8,128)(2,1)}, u32[]{:S(2)}, u32[]{:S(2)}) %collective-permute-start.3) | collective-permute-done | bytes 1048608 | tf_op jit(solution)/shard_map/ppermute | solution.py:20
  356.8 1.7 pad_maximum_fusion.3
  358.5 3.9 copy.11
  362.5 3.0 bitcast_select_fusion
  365.5 6.3 %fusion.17 = f32[1024,896]{0,1:T(8,128)} fusion(bf16[1024,1024]{1,0:T(8,128)(2,1)S(1)} %bitcast_select_fusion, bf16[1024,1792]{1,0:T(8,128)(2,1)} %collective-permute-done.2), kind=kOutput, calls=%fused_computation.32 | convolution fusion | flops 1879048192 | bytes 7602176 | tf_op jit(solution)/shard_map/dot_general | solution.py:89
  371.8 5.7 %fusion.19 = f32[1024,896]{0,1:T(8,128)} fusion(bf16[1024,1024]{1,0:T(8,128)(2,1)S(1)} %copy-done.13, bf16[1024,1792]{1,0:T(8,128)(2,1)} %collective-permute-done), kind=kOutput, calls=%fused_computation.34 | convolution fusion | flops 1879048192 | bytes 7602176 | tf_op jit(solution)/shard_map/dot_general | solution.py:89
  377.6 18.3 %fusion.75 = (bf16[1024,896]{0,1:T(8,128)(2,1)}, f32[1024,896]{0,1:T(8,128)S(1)}) fusion(bf16[1024,1024]{1,0:T(8,128)(2,1)S(1)} %broadcast_select_fusion, bf16[1024,1792]{1,0:T(8,128)(2,1)S(1)} %copy-done.7, f32[1024,896]{0,1:T(8,128)} %fusion.17, f32[1024,896]{0,1:T(8,128)} %fusion.19, f32[1024,896]{0,1:T(8,128)S(1)} %copy-done.8, f32[1024]{0:T(1024)S(1)} %psum.7, ...), kind=kOutput, calls=%fused_computation.79 | convolution fusion | flops 1887305728 | bytes 24121344 | tf_op jit(solution)/shard_map/dot_general | solution.py:89
  395.9 1.5 collective-permute-start.8
  397.5 1.5 collective-permute-start.7
  398.9 6.1 %fusion.11 = f32[1024,896]{0,1:T(8,128)} fusion(bf16[1024,1024]{1,0:T(8,128)(2,1)} %copy-done.15, bf16[1024,1792]{1,0:T(8,128)(2,1)} %collective-permute-done.2), kind=kOutput, calls=%fused_computation.26 | convolution fusion | flops 1879048192 | bytes 7602176 | tf_op jit(solution)/shard_map/dot_general | solution.py:89
  405.0 5.5 %fusion.13 = f32[1024,896]{0,1:T(8,128)} fusion(bf16[1024,1024]{1,0:T(8,128)(2,1)S(1)} %copy-done.13, bf16[1024,1792]{1,0:T(8,128)(2,1)} %collective-permute-done), kind=kOutput, calls=%fused_computation.28 | convolution fusion | flops 1879048192 | bytes 7602176 | tf_op jit(solution)/shard_map/dot_general | solution.py:89
  410.5 6.9 %fusion.74 = (bf16[1024,896]{0,1:T(8,128)(2,1)}, f32[1024,896]{0,1:T(8,128)S(1)}) fusion(bf16[1024,1024]{1,0:T(8,128)(2,1)S(1)} %broadcast_select_fusion, bf16[1024,1792]{1,0:T(8,128)(2,1)S(1)} %copy-done.7, f32[1024,896]{0,1:T(8,128)} %fusion.11, f32[1024,896]{0,1:T(8,128)} %fusion.13, f32[1024,896]{0,1:T(8,128)} %fusion.33, f32[1024]{0:T(1024)S(1)} %psum.7, ...), kind=kOutput, calls=%fused_computation.78 | convolution fusion | flops 1887305728 | bytes 24121344 | tf_op jit(solution)/shard_map/dot_general | solution.py:89
  418.6 5.1 fusion.71
  423.7 2.1 fusion.72
  425.7 13.5 %collective-permute-done.8 = bf16[1024,896]{0,1:T(8,128)(2,1)} collective-permute-done((bf16[1024,896]{0,1:T(8,128)(2,1)}, bf16[1024,896]{0,1:T(8,128)(2,1)}, u32[]{:S(2)}, u32[]{:S(2)}) %collective-permute-start.8) | collective-permute-done | bytes 1835040 | tf_op jit(solution)/shard_map/ppermute | solution.py:20
  440.5 1.5 collective-permute-start.10
  443.3 1.6 collective-permute-start.9
  444.8 33.7 %collective-permute-done.12 = bf16[1024,896]{0,1:T(8,128)(2,1)S(1)} collective-permute-done((bf16[1024,896]{0,1:T(8,128)(2,1)}, bf16[1024,896]{0,1:T(8,128)(2,1)S(1)}, u32[]{:S(2)}, u32[]{:S(2)}) %collective-permute-start.12) | collective-permute-done | bytes 1835040 | tf_op jit(solution)/shard_map/ppermute | solution.py:20
  478.6 1.5 collective-permute-start.14
  481.1 1.5 collective-permute-start.13
  482.6 5.5 %fusion.77 = f32[1024,896]{0,1:T(8,128)} fusion(bf16[1024,1024]{1,0:T(8,128)(2,1)S(1)} %copy-done.16, bf16[1024,896]{0,1:T(8,128)(2,1)} %collective-permute-done.8), kind=kOutput, calls=%fused_computation.81 | convolution fusion | flops 1879048192 | bytes 7602176 | tf_op jit(solution)/shard_map/dot_general | solution.py:89
  488.1 5.5 %fusion.76 = f32[1024,896]{0,1:T(8,128)} fusion(bf16[1024,1024]{1,0:T(8,128)(2,1)S(1)} %copy-done.14, bf16[1024,896]{0,1:T(8,128)(2,1)} %collective-permute-done.7), kind=kOutput, calls=%fused_computation.80 | convolution fusion | flops 1879048192 | bytes 7602176 | tf_op jit(solution)/shard_map/dot_general | solution.py:89
  493.6 3.9 fusion.79
  497.6 3.9 fusion.78
  503.4 8.0 %multiply_convert_fusion.1 = bf16[1024,896]{0,1:T(8,128)(2,1)S(1)} fusion(f32[1024,896]{0,1:T(8,128)} %fusion.77, f32[1024,896]{0,1:T(8,128)} %fusion.76, f32[1024,896]{0,1:T(8,128)} %fusion.71, f32[1024,896]{0,1:T(8,128)S(1)} %get-tuple-element.22, f32[1024,1792]{0,1:T(8,128)S(1)} %bitcast.29, bf16[1024,1024]{1,0:T(8,128)(2,1)S(1)} %broadcast_select_fusion, ...), kind=kOutput, calls=%fused_computation.6 | convolution fusion | flops 1890975744 | bytes 24121344 | tf_op jit(solution)/shard_map/dot_general | solution.py:89
  511.3 5.5 %collective-permute-done.14 = bf16[512,896]{0,1:T(8,128)(2,1)} collective-permute-done((bf16[512,896]{0,1:T(8,128)(2,1)S(1)}, bf16[512,896]{0,1:T(8,128)(2,1)}, u32[]{:S(2)}, u32[]{:S(2)}) %collective-permute-start.14) | collective-permute-done | bytes 917536 | tf_op jit(solution)/shard_map/ppermute | solution.py:20
  516.9 6.8 %multiply_convert_fusion = bf16[1024,896]{0,1:T(8,128)(2,1)S(1)} fusion(f32[1024,896]{0,1:T(8,128)} %fusion.79, f32[1024,896]{0,1:T(8,128)} %fusion.78, f32[1024,896]{0,1:T(8,128)S(1)} %fusion.72, f32[1024,896]{0,1:T(8,128)S(1)} %get-tuple-element.20, f32[1024,1792]{0,1:T(8,128)S(1)} %bitcast.29, bf16[1024,1024]{1,0:T(8,128)(2,1)S(1)} %broadcast_select_fusion, ...), kind=kOutput, calls=%fused_computation.4 | convolution fusion | flops 1890975744 | bytes 24121344 | tf_op jit(solution)/shard_map/dot_general | solution.py:89
  523.7 2.2 pad_maximum_fusion
  525.9 5.9 %copy.13 = bf16[1024,1792]{1,0:T(8,128)(2,1)} copy(bf16[1024,1792]{0,1:T(8,128)(2,1)} %pad_maximum_fusion) | data formatting | bytes 7340032 | tf_op jit(solution)/shard_map/concatenate | solution.py:102
  (107 shorter events, 19.1 us)
Async XLA Ops:
  6.5 47.2 %reduce-scatter.13.cloned.1.call-start = ((), (), s32[]{:S(2)}) async-start(), calls=%async_computation.11 | async-start | bytes 1966080
  15.5 91.7 %all-gather.5.cloned.1.call-start = ((), (), s32[]{:S(2)}) async-start(), calls=%async_computation.4 | async-start | bytes 1966080 | tf_op jit(solution)/shard_map/all_gather | solution.py:46
  15.6 82.7 %collective-permute-start = (bf16[1024,1792]{1,0:T(8,128)(2,1)}, bf16[1024,1792]{1,0:T(8,128)(2,1)}, u32[]{:S(2)}, u32[]{:S(2)}) collective-permute-start(bf16[1024,1792]{1,0:T(8,128)(2,1)} %param.1), channel_id=1, source_target_pairs={{0,4},{4,0},{8,12},{12,8},{1,5},{5,1},{9,13},{13,9},{2,6},{6,2},{1... | collective-permute-start | bytes 11010056 | tf_op jit(solution)/shard_map/ppermute | solution.py:20
  18.6 84.3 %collective-permute-start.2 = (bf16[1024,1792]{1,0:T(8,128)(2,1)}, bf16[1024,1792]{1,0:T(8,128)(2,1)}, u32[]{:S(2)}, u32[]{:S(2)}) collective-permute-start(bf16[1024,1792]{1,0:T(8,128)(2,1)} %param.1), channel_id=1, source_target_pairs={{0,8},{4,12},{8,0},{12,4},{1,9},{5,13},{9,1},{13,5},{2,10},{6,14},... | collective-permute-start | bytes 11010056 | tf_op jit(solution)/shard_map/ppermute | solution.py:20
  55.6 131.3 %reduce-scatter.11.cloned.1.call-start = ((), (), s32[]{:S(2)}) async-start(), calls=%async_computation.9 | async-start | bytes 1310720 | tf_op jit(solution)/shard_map/reduce_scatter | solution.py:45
  101.1 41.4 %collective-permute-start.4 = (bf16[512,1792]{1,0:T(8,128)(2,1)}, bf16[512,1792]{1,0:T(8,128)(2,1)S(1)}, u32[]{:S(2)}, u32[]{:S(2)}) collective-permute-start(bf16[512,1792]{1,0:T(8,128)(2,1)} %slice.112), channel_id=1, source_target_pairs={{0,8},{4,12},{8,0},{12,4},{1,9},{5,13},{9,1},{13,5},{2,10},{6,14},... | collective-permute-start | bytes 5505032 | tf_op jit(solution)/shard_map/ppermute | solution.py:20
  105.8 42.7 %collective-permute-start.5 = (bf16[512,1792]{1,0:T(8,128)(2,1)}, bf16[512,1792]{1,0:T(8,128)(2,1)}, u32[]{:S(2)}, u32[]{:S(2)}) collective-permute-start(bf16[512,1792]{1,0:T(8,128)(2,1)} %slice.113), channel_id=1, source_target_pairs={{0,4},{4,0},{8,12},{12,8},{1,5},{5,1},{9,13},{13,9},{2,6},{6,2},{1... | collective-permute-start | bytes 5505032 | tf_op jit(solution)/shard_map/ppermute | solution.py:20
  113.5 30.3 %copy-start.9 = (bf16[1024,1792]{1,0:T(8,128)(2,1)S(1)}, bf16[1024,1792]{1,0:T(8,128)(2,1)}, u32[]{:S(2)}) copy-start(bf16[1024,1792]{1,0:T(8,128)(2,1)} %param.1) | copy-start | bytes 11010052
  148.5 3.0 copy-start.10
  156.2 58.8 %reduce-scatter.7.cloned.1.call-start = ((), (), s32[]{:S(2)}) async-start(), calls=%async_computation.5 | async-start | bytes 1310720 | tf_op jit(solution)/shard_map/reduce_scatter | solution.py:45
  156.7 86.2 %reduce-scatter.9.cloned.1.call-start = ((), (), s32[]{:S(2)}) async-start(), calls=%async_computation.7 | async-start | bytes 1310720 | tf_op jit(solution)/shard_map/reduce_scatter | solution.py:45
  157.3 113.8 %all-gather.11.cloned.1.call-start = ((), (), s32[]{:S(2)}) async-start(), calls=%async_computation.10 | async-start | bytes 1310720 | tf_op jit(solution)/shard_map/all_gather | solution.py:46
  187.0 113.3 %all-gather.7.cloned.1.call-start = ((), (), s32[]{:S(2)}) async-start(), calls=%async_computation.6 | async-start | bytes 1310720 | tf_op jit(solution)/shard_map/all_gather | solution.py:46
  215.0 114.3 %all-gather.9.cloned.1.call-start = ((), (), s32[]{:S(2)}) async-start(), calls=%async_computation.8 | async-start | bytes 1310720 | tf_op jit(solution)/shard_map/all_gather | solution.py:46
  227.0 46.5 %copy-start.12 = (bf16[512,1536]{0,1:T(8,128)(2,1)S(1)}, bf16[512,1536]{0,1:T(8,128)(2,1)}, u32[]{:S(2)}) copy-start(bf16[512,1536]{0,1:T(8,128)(2,1)} %all-gather.5.cloned.1.call-done) | copy-start | bytes 4718596
  271.2 59.7 %collective-permute-start.6 = (bf16[512,1024]{1,0:T(8,128)(2,1)}, bf16[512,1024]{1,0:T(8,128)(2,1)}, u32[]{:S(2)}, u32[]{:S(2)}) collective-permute-start(bf16[512,1024]{1,0:T(8,128)(2,1)} %all-gather.11.cloned.1.call-done), channel_id=1, source_target_pairs={{0,12},{4,8},{8,4},{12,0},{1,13},{5,9},{9,5},{13,1},{2,14},{6,10},... | collective-permute-start | bytes 3145736 | tf_op jit(solution)/shard_map/ppermute | solution.py:20
  274.6 32.9 %copy-start.25 = (bf16[512,512]{1,0:T(8,128)(2,1)}, bf16[512,512]{1,0:T(8,128)(2,1)S(1)}, u32[]{:S(2)}) copy-start(bf16[512,512]{1,0:T(8,128)(2,1)S(1)} %copy.16) | copy-start | bytes 1572868
  274.7 32.8 %copy-start.21 = (bf16[512,1024]{0,1:T(8,128)(2,1)}, bf16[512,1024]{0,1:T(8,128)(2,1)S(1)}, u32[]{:S(2)}) copy-start(bf16[512,1024]{0,1:T(8,128)(2,1)S(1)} %slice.109) | copy-start | bytes 3145732
  300.3 35.8 %collective-permute-start.1 = (bf16[512,1024]{1,0:T(8,128)(2,1)}, bf16[512,1024]{1,0:T(8,128)(2,1)}, u32[]{:S(2)}, u32[]{:S(2)}) collective-permute-start(bf16[512,1024]{1,0:T(8,128)(2,1)} %all-gather.7.cloned.1.call-done), channel_id=1, source_target_pairs={{0,4},{4,0},{8,12},{12,8},{1,5},{5,1},{9,13},{13,9},{2,6},{6,2},{1... | collective-permute-start | bytes 3145736 | tf_op jit(solution)/shard_map/ppermute | solution.py:20
  301.7 5.7 %copy-start.11 = (bf16[1024,1792]{1,0:T(8,128)(2,1)S(1)}, bf16[1024,1792]{1,0:T(8,128)(2,1)}, u32[]{:S(2)}) copy-start(bf16[1024,1792]{1,0:T(8,128)(2,1)} %param.1) | copy-start | bytes 11010052
  301.7 5.7 %copy-start.27 = (bf16[512,512]{0,1:T(8,128)(2,1)S(1)}, bf16[512,512]{0,1:T(8,128)(2,1)}, u32[]{:S(2)}) copy-start(bf16[512,512]{0,1:T(8,128)(2,1)} %get-tuple-element.17) | copy-start | bytes 1572868
  307.5 23.4 %copy-start.20 = (bf16[512,1024]{1,0:T(8,128)(2,1)S(1)}, bf16[512,1024]{1,0:T(8,128)(2,1)}, u32[]{:S(2)}) copy-start(bf16[512,1024]{1,0:T(8,128)(2,1)} %all-gather.11.cloned.1.call-done) | copy-start | bytes 3145732
  329.4 25.1 %collective-permute-start.3 = (bf16[512,1024]{1,0:T(8,128)(2,1)}, bf16[512,1024]{1,0:T(8,128)(2,1)}, u32[]{:S(2)}, u32[]{:S(2)}) collective-permute-start(bf16[512,1024]{1,0:T(8,128)(2,1)} %all-gather.9.cloned.1.call-done), channel_id=1, source_target_pairs={{0,8},{4,12},{8,0},{12,4},{1,9},{5,13},{9,1},{13,5},{2,10},{6,14},... | collective-permute-start | bytes 3145736 | tf_op jit(solution)/shard_map/ppermute | solution.py:20
  332.2 1.0 copy-start
  337.7 1.1 copy-start.1
  337.7 1.4 copy-start.3
  342.0 3.0 copy-start.2
  342.0 3.0 copy-start.4
  342.0 3.2 copy-start.6
  345.1 9.3 %copy-start.19 = (bf16[512,1024]{1,0:T(8,128)(2,1)S(1)}, bf16[512,1024]{1,0:T(8,128)(2,1)}, u32[]{:S(2)}) copy-start(bf16[512,1024]{1,0:T(8,128)(2,1)} %all-gather.9.cloned.1.call-done) | copy-start | bytes 3145732
  355.8 1.0 copy-start.5
  362.4 15.1 %slice-start = ((s8[7340032]{0:T(1024)(128)(4,1)}), s8[4194304]{0:T(1024)(128)(4,1)S(1)}, s32[]{:S(2)}) async-start(s8[7340032]{0:T(1024)(128)(4,1)} %bitcast.28), calls=%async_computation.12 | async-start | bytes 8388608
  365.5 6.4 %copy-start.15 = (bf16[1024,1024]{1,0:T(8,128)(2,1)}, bf16[1024,1024]{1,0:T(8,128)(2,1)S(1)}, u32[]{:S(2)}) copy-start(bf16[1024,1024]{1,0:T(8,128)(2,1)S(1)} %bitcast_select_fusion) | copy-start | bytes 6291460
  365.5 6.3 %copy-start.13 = (bf16[1024,1024]{1,0:T(8,128)(2,1)S(1)}, bf16[1024,1024]{1,0:T(8,128)(2,1)}, u32[]{:S(2)}) copy-start(bf16[1024,1024]{1,0:T(8,128)(2,1)} %bitcast_select_fusion.1) | copy-start | bytes 6291460
  365.5 12.1 %slice-start.1 = ((s8[7340032]{0:T(1024)(128)(4,1)}), s8[3145728]{0:T(1024)(128)(4,1)S(1)}, s32[]{:S(2)}) async-start(s8[7340032]{0:T(1024)(128)(4,1)} %bitcast.28), calls=%async_computation.13 | async-start | bytes 6291456
  371.8 5.7 %copy-start.7 = (bf16[1024,1792]{1,0:T(8,128)(2,1)S(1)}, bf16[1024,1792]{1,0:T(8,128)(2,1)}, u32[]{:S(2)}) copy-start(bf16[1024,1792]{1,0:T(8,128)(2,1)} %constant_dynamic-update-slice_fusion) | copy-start | bytes 11010052
  371.8 5.7 %copy-start.8 = (f32[1024,896]{0,1:T(8,128)S(1)}, f32[1024,896]{0,1:T(8,128)}, u32[]{:S(2)}) copy-start(f32[1024,896]{0,1:T(8,128)} %fusion.41) | copy-start | bytes 11010052
  395.9 43.3 %collective-permute-start.8 = (bf16[1024,896]{0,1:T(8,128)(2,1)}, bf16[1024,896]{0,1:T(8,128)(2,1)}, u32[]{:S(2)}, u32[]{:S(2)}) collective-permute-start(bf16[1024,896]{0,1:T(8,128)(2,1)} %get-tuple-element.21), channel_id=1, source_target_pairs={{0,8},{4,12},{8,0},{12,4},{1,9},{5,13},{9,1},{13,5},{2,10},{6,14},... | collective-permute-start | bytes 5505032 | tf_op jit(solution)/shard_map/ppermute | solution.py:20
  397.5 44.6 %collective-permute-start.7 = (bf16[1024,896]{0,1:T(8,128)(2,1)}, bf16[1024,896]{0,1:T(8,128)(2,1)}, u32[]{:S(2)}, u32[]{:S(2)}) collective-permute-start(bf16[1024,896]{0,1:T(8,128)(2,1)} %get-tuple-element.21), channel_id=1, source_target_pairs={{0,4},{4,0},{8,12},{12,8},{1,5},{5,1},{9,13},{13,9},{2,6},{6,2},{1... | collective-permute-start | bytes 5505032 | tf_op jit(solution)/shard_map/ppermute | solution.py:20
  410.5 8.1 %copy-start.17 = (bf16[1024,896]{0,1:T(8,128)(2,1)S(1)}, bf16[1024,896]{0,1:T(8,128)(2,1)}, u32[]{:S(2)}) copy-start(bf16[1024,896]{0,1:T(8,128)(2,1)} %get-tuple-element.21) | copy-start | bytes 5505028
  410.5 8.1 %copy-start.22 = (bf16[512,1024]{0,1:T(8,128)(2,1)S(1)}, bf16[512,1024]{0,1:T(8,128)(2,1)}, u32[]{:S(2)}) copy-start(bf16[512,1024]{0,1:T(8,128)(2,1)} %copy-done.21) | copy-start | bytes 3145732
  417.4 6.2 %copy-start.18 = (bf16[1024,896]{0,1:T(8,128)(2,1)S(1)}, bf16[1024,896]{0,1:T(8,128)(2,1)}, u32[]{:S(2)}) copy-start(bf16[1024,896]{0,1:T(8,128)(2,1)} %get-tuple-element.19) | copy-start | bytes 5505028
  417.4 6.2 %copy-start.26 = (bf16[512,512]{1,0:T(8,128)(2,1)S(1)}, bf16[512,512]{1,0:T(8,128)(2,1)}, u32[]{:S(2)}) copy-start(bf16[512,512]{1,0:T(8,128)(2,1)} %copy-done.25) | copy-start | bytes 1572868
  417.4 6.2 %copy-start.28 = (bf16[512,512]{0,1:T(8,128)(2,1)S(1)}, bf16[512,512]{0,1:T(8,128)(2,1)}, u32[]{:S(2)}) copy-start(bf16[512,512]{0,1:T(8,128)(2,1)} %get-tuple-element.17) | copy-start | bytes 1572868
  417.4 61.1 %collective-permute-start.12 = (bf16[1024,896]{0,1:T(8,128)(2,1)}, bf16[1024,896]{0,1:T(8,128)(2,1)S(1)}, u32[]{:S(2)}, u32[]{:S(2)}) collective-permute-start(bf16[1024,896]{0,1:T(8,128)(2,1)} %get-tuple-element.19), channel_id=1, source_target_pairs={{0,8},{4,12},{8,0},{12,4},{1,9},{5,13},{9,1},{13,5},{2,10},{6,14},... | collective-permute-start | bytes 5505032 | tf_op jit(solution)/shard_map/ppermute | solution.py:20
  418.0 62.1 %collective-permute-start.11 = (bf16[1024,896]{0,1:T(8,128)(2,1)}, bf16[1024,896]{0,1:T(8,128)(2,1)S(1)}, u32[]{:S(2)}, u32[]{:S(2)}) collective-permute-start(bf16[1024,896]{0,1:T(8,128)(2,1)} %get-tuple-element.19), channel_id=1, source_target_pairs={{0,4},{4,0},{8,12},{12,8},{1,5},{5,1},{9,13},{13,9},{2,6},{6,2},{1... | collective-permute-start | bytes 5505032 | tf_op jit(solution)/shard_map/ppermute | solution.py:20
  425.7 56.9 %copy-start.16 = (bf16[1024,1024]{1,0:T(8,128)(2,1)S(1)}, bf16[1024,1024]{1,0:T(8,128)(2,1)}, u32[]{:S(2)}) copy-start(bf16[1024,1024]{1,0:T(8,128)(2,1)} %copy-done.15) | copy-start | bytes 6291460
  440.5 61.0 %collective-permute-start.10 = (bf16[512,896]{0,1:T(8,128)(2,1)S(1)}, bf16[512,896]{0,1:T(8,128)(2,1)S(1)}, u32[]{:S(2)}, u32[]{:S(2)}) collective-permute-start(bf16[512,896]{0,1:T(8,128)(2,1)S(1)} %slice.116), channel_id=1, source_target_pairs={{0,4},{4,0},{8,12},{12,8},{1,5},{5,1},{9,13},{13,9},{2,6},{6,2},{1... | collective-permute-start | bytes 2752520 | tf_op jit(solution)/shard_map/ppermute | solution.py:20
  443.3 58.2 %collective-permute-start.9 = (bf16[512,896]{0,1:T(8,128)(2,1)S(1)}, bf16[512,896]{0,1:T(8,128)(2,1)S(1)}, u32[]{:S(2)}, u32[]{:S(2)}) collective-permute-start(bf16[512,896]{0,1:T(8,128)(2,1)S(1)} %slice.115), channel_id=1, source_target_pairs={{0,8},{4,12},{8,0},{12,4},{1,9},{5,13},{9,1},{13,5},{2,10},{6,14},... | collective-permute-start | bytes 2752520 | tf_op jit(solution)/shard_map/ppermute | solution.py:20
  478.6 38.3 %collective-permute-start.14 = (bf16[512,896]{0,1:T(8,128)(2,1)S(1)}, bf16[512,896]{0,1:T(8,128)(2,1)}, u32[]{:S(2)}, u32[]{:S(2)}) collective-permute-start(bf16[512,896]{0,1:T(8,128)(2,1)S(1)} %slice.122), channel_id=1, source_target_pairs={{0,4},{4,0},{8,12},{12,8},{1,5},{5,1},{9,13},{13,9},{2,6},{6,2},{1... | collective-permute-start | bytes 2752520 | tf_op jit(solution)/shard_map/ppermute | solution.py:20
  481.1 7.0 %copy-start.14 = (bf16[1024,1024]{1,0:T(8,128)(2,1)S(1)}, bf16[1024,1024]{1,0:T(8,128)(2,1)}, u32[]{:S(2)}) copy-start(bf16[1024,1024]{1,0:T(8,128)(2,1)} %bitcast_select_fusion.1) | copy-start | bytes 6291460
  481.1 35.8 %collective-permute-start.13 = (bf16[512,896]{0,1:T(8,128)(2,1)}, bf16[512,896]{0,1:T(8,128)(2,1)}, u32[]{:S(2)}, u32[]{:S(2)}) collective-permute-start(bf16[512,896]{0,1:T(8,128)(2,1)} %slice.121), channel_id=1, source_target_pairs={{0,8},{4,12},{8,0},{12,4},{1,9},{5,13},{9,1},{13,5},{2,10},{6,14},... | collective-permute-start | bytes 2752520 | tf_op jit(solution)/shard_map/ppermute | solution.py:20
  501.5 0.9 copy-start.23
  502.4 0.9 copy-start.24
Sparse Core Ops, SparseCore 0:
  15.7 37.9 reduce-scatter.12
  55.8 36.6 all-gather.4
  156.3 30.6 reduce-scatter.10
  189.2 25.7 reduce-scatter.6
  217.2 25.7 reduce-scatter.8
  244.5 26.6 all-gather.10
  272.8 27.4 all-gather.6
  301.9 27.4 all-gather.8

commit v5 on v4

--- a/solution.py
+++ b/solution.py
@@ -69,19 +69,33 @@
             axis=0,
         )
     ]
+    direct = [offset for offset in range(1, count) if offset & (offset - 1) == 0]
+    distant = [offset for offset in range(1, count) if offset & (offset - 1) != 0]
+    found = {}
     before = packed
-    for offset in range(1, count):
-        lower = (me & (1 << (offset.bit_length() - 1))) == 0
-        before, other = lax.optimization_barrier((before, blocks[offset]))
-        tall = jnp.where(lower, iterate, other)
-        short = jnp.where(lower, other[:half], iterate[half:])
-        before = times_transpose(short, tall).astype(jnp.bfloat16)
-        mine = sum_over_columns(before)
-        theirs = swap(mine, offset, count)
-        pair = jnp.concatenate(
-            [jnp.where(lower, mine, theirs), jnp.where(lower, theirs, mine)], axis=0
+    for offsets in (direct, distant):
+        partials = []
+        for offset in offsets:
+            lower = (me & (1 << (offset.bit_length() - 1))) == 0
+            other = lax.optimization_barrier((before, blocks[offset]))[1]
+            tall = jnp.where(lower, iterate, other)
+            short = jnp.where(lower, other[:half], iterate[half:])
+            partials.append(times_transpose(short, tall).astype(jnp.bfloat16))
+        if not partials:
+            continue
+        before = lax.psum_scatter(
+            jnp.concatenate(partials, axis=1), "col", scatter_dimension=0, tiled=True
         )
-        gram.append(jnp.where(lower, pair.T, pair))
+        summed = lax.all_gather(before, "col", axis=0, tiled=True)
+        for at, offset in enumerate(offsets):
+            lower = (me & (1 << (offset.bit_length() - 1))) == 0
+            mine = summed[:, at * rows : (at + 1) * rows]
+            theirs = swap(mine, offset, count)
+            pair = jnp.concatenate(
+                [jnp.where(lower, mine, theirs), jnp.where(lower, theirs, mine)], axis=0
+            )
+            found[offset] = jnp.where(lower, pair.T, pair)
+    gram += [found[offset] for offset in range(1, count)]
 
     def apply_gram(own, parts):
         total = diagonal * own

time: 541 us -> 485 us (0.90)
  waiting for transfers between devices: 298 us -> 245 us
  local copies, waits for them, and re-layouts: 44.9 us -> 55.5 us
  matrix products: 122 us -> 112 us
    all_gather x4 -> x1, waiting for transfers between devices: 58.7 us -> 0.01 us  [sum_over_columns(): return lax.all_gather(owned, 'col', axis=0, tiled=True)]
    reduce_scatter x3 -> x2, waiting for transfers between devices: 73.5 us -> 22.1 us  [shards(): lax.psum_scatter(jnp.concatenate(partials, axis=1), 'col', scatter_dimens...]
    all_gather x0 -> x2, waiting for transfers between devices: none -> 39.4 us  [shards(): summed = lax.all_gather(before, 'col', axis=0, tiled=True)]
    ppermute x15, waiting for transfers between devices: 131 us -> 149 us  [swap(): return lax.ppermute(block, 'row', [(i, i ^ offset) for i in range(count)])]
    transpose x1, local copies, waits for them, and re-layouts: 2.58 us -> 15 us  [shards(): found[offset] = jnp.where(lower, pair.T, pair)]
    dot_general x16, matrix products: 99.4 us -> 90.1 us  [apply_gram(): total = total + jnp.dot(block, part, preferred_element_type=jnp.float32)]
    unnamed x67 -> x55, local copies, waits for them, and re-layouts: 16.5 us -> 15.3 us
    unnamed x9 -> x7, waiting for transfers between devices: 34.7 us -> 34.2 us
  transfers between devices with their start and end apart: 23 -> 21, of which waited for: 13 -> 11; matrix products, arithmetic and copies ran while one was open for 21% -> 25% of each run, Pallas kernels for 0% -> 0%
where the time goes in v5:
time: 485 us; the launch traced here: 482 us
  waiting for transfers between devices  245 us (51%)
  matrix products  112 us (23%)
  local copies, waits for them, and re-layouts  55.5 us (11%)
  other arithmetic  25 us (5%)
  starting transfers between devices  19.9 us (4%)
  between operations  14 us (3%)
  blocking collectives  10.2 us (2%)
    ppermute x15, waiting for transfers between devices, swap(): return lax.ppermute(block, 'row', [(i, i ^ offset) for i in range(count)])  149 us
    dot_general x16, matrix products, apply_gram(): total = total + jnp.dot(block, part, preferred_element_type=jnp.float32)  90.1 us
    all_gather x2, waiting for transfers between devices, shards(): summed = lax.all_gather(before, 'col', axis=0, tiled=True)  39.4 us
    unnamed x7, waiting for transfers between devices  34.2 us
    dot_general x4, matrix products, times_transpose(): lax.dot_general(left, right, (((1,), (1,)), ((), ())), preferred_element_...  22.3 us
    reduce_scatter x2, waiting for transfers between devices, shards(): lax.psum_scatter(jnp.concatenate(partials, axis=1), 'col', scatter_dimens...  22.1 us
    ppermute x15, starting transfers between devices, swap(): return lax.ppermute(block, 'row', [(i, i ^ offset) for i in range(count)])  19.7 us
    unnamed x55, local copies, waits for them, and re-layouts  15.3 us
  transfers between devices with their start and end apart: 21, of which 11 were waited for; matrix products, arithmetic and copies ran while one was open for 25% of the time, Pallas kernels for 0%

profile of v5, /device:TPU:0, one launch (start us, length us, event | category | flops | bytes accessed | tf_op | source)
XLA Modules:
  0.0 481.6 jit_solution(5718025751058859666)
XLA Ops:
  6.5 7.1 %select_convert_fusion = bf16[1024,1024]{0,1:T(8,128)(2,1)S(1)} fusion(bf16[1024,1792]{1,0:T(8,128)(2,1)} %param.1), kind=kOutput, calls=%fused_computation.1 | convolution fusion | flops 3761242112 | bytes 5767168 | tf_op jit(solution)/shard_map/dot_general | solution.py:39
  13.9 1.6 copy.14
  15.6 3.0 collective-permute-start.1
  18.6 1.5 collective-permute-start
  20.1 33.6 %reduce-scatter.10.cloned.1.call-done = bf16[128,1536]{1,0:T(8,128)(2,1)} async-done(((bf16[512,1536]{1,0:T(8,128)(2,1)}), bf16[128,1536]{1,0:T(8,128)(2,1)}) %reduce-scatter.10.cloned.1.call-update) | async-done | bytes 393232
  53.7 1.9 copy.15
  55.7 42.6 %collective-permute-done.1 = bf16[1024,1792]{1,0:T(8,128)(2,1)} collective-permute-done((bf16[1024,1792]{1,0:T(8,128)(2,1)}, bf16[1024,1792]{1,0:T(8,128)(2,1)}, u32[]{:S(2)}, u32[]{:S(2)}) %collective-permute-start.1) | collective-permute-done | bytes 3670048 | tf_op jit(solution)/shard_map/ppermute | solution.py:20
  98.3 1.5 collective-permute-done
  99.7 5.2 %fusion.55 = bf16[512,1024]{1,0:T(8,128)(2,1)S(1)} fusion(bf16[1024,1792]{1,0:T(8,128)(2,1)} %param.1, bf16[1024,1792]{1,0:T(8,128)(2,1)} %collective-permute-done.1, pred[]{:T(512)S(6)} %eq.15), kind=kOutput, calls=%fused_computation.60 | convolution fusion | flops 1882324992 | bytes 12059648 | tf_op jit(solution)/shard_map/dot_general | solution.py:39
  105.0 3.6 fusion.50
  108.7 1.5 pad_maximum_fusion.2
  110.2 1.6 slice.122
  112.4 1.6 slice.123
  114.0 2.8 collective-permute-start.5
  116.8 35.9 %collective-permute-done.4 = bf16[512,1792]{1,0:T(8,128)(2,1)S(1)} collective-permute-done((bf16[512,1792]{1,0:T(8,128)(2,1)S(1)}, bf16[512,1792]{1,0:T(8,128)(2,1)S(1)}, u32[]{:S(2)}, u32[]{:S(2)}) %collective-permute-start.4) | collective-permute-done | bytes 1835040 | tf_op jit(solution)/shard_map/ppermute | solution.py:20
  152.7 1.3 constant_dynamic-update-slice_fusion.1
  154.1 1.4 collective-permute-done.5
  155.5 1.3 constant_dynamic-update-slice_fusion
  156.8 6.2 %fusion.60 = bf16[512,1024]{1,0:T(8,128)(2,1)} fusion(bf16[1024,1792]{1,0:T(8,128)(2,1)} %param.1, bf16[1024,1792]{1,0:T(8,128)(2,1)} %constant_dynamic-update-slice_fusion, pred[]{:T(512)S(6)} %eq.15), kind=kOutput, calls=%fused_computation.61 | convolution fusion | flops 1882324992 | bytes 12059648 | tf_op jit(solution)/shard_map/dot_general | solution.py:39
  163.7 6.0 %copy.8 = bf16[1024,1792]{0,1:T(8,128)(2,1)} copy(bf16[1024,1792]{1,0:T(8,128)(2,1)} %param.1) | data formatting | bytes 7340032 | tf_op args[0]
  169.7 22.1 %reduce-scatter.8.cloned.1.call-done = bf16[128,1024]{1,0:T(8,128)(2,1)} async-done(((bf16[512,1024]{1,0:T(8,128)(2,1)}), bf16[128,1024]{1,0:T(8,128)(2,1)}) %reduce-scatter.8.cloned.1.call-update) | async-done | bytes 262160 | tf_op jit(solution)/shard_map/reduce_scatter | solution.py:86
  191.9 3.1 multiply_reduce_fusion
  195.0 3.8 convert_element_type.25
  198.8 10.2 %psum.7 = f32[1024]{0:T(1024)S(1)} all-reduce(f32[1024]{0:T(1024)S(1)} %multiply_reduce_fusion), channel_id=1, replica_groups=mesh['grp'=2,'row'=4,'col'=4] {'col'}, use_global_device_ids=true, to_apply=%region_1.0 | all-reduce | flops 1024 | bytes 8192 | tf_op jit(solution)/shard_map/psum | solution.py:57
  208.9 29.2 %all-gather.6.cloned.1.call-done = bf16[512,2048]{1,0:T(8,128)(2,1)} async-done(((bf16[128,2048]{1,0:T(8,128)(2,1)}), bf16[512,2048]{1,0:T(8,128)(2,1)}) %all-gather.6.cloned.1.call-update) | async-done | bytes 2097168 | tf_op jit(solution)/shard_map/all_gather | solution.py:89
  238.2 3.0 fusion.73
  241.2 1.5 collective-permute-start.2
  242.7 1.5 collective-permute-start.3
  246.1 6.2 %fusion.33 = f32[1024,896]{0,1:T(8,128)} fusion(bf16[1024,1792]{1,0:T(8,128)(2,1)} %param.1, bf16[512,1024]{0,1:T(8,128)(2,1)S(1)} %slice.117, bf16[512,512]{0,1:T(8,128)(2,1)} %bitcast.30, bf16[512,512]{0,1:T(8,128)(2,1)} %get-tuple-element.21), kind=kOutput, calls=%fused_computation.45 | convolution fusion | flops 1885339648 | bytes 7602176 | tf_op jit(solution)/shard_map/dot_general | solution.py:103
  252.3 4.0 fusion.41
  256.4 10.2 %all-gather.8.cloned.1.call-done = bf16[512,1024]{1,0:T(8,128)(2,1)} async-done(((bf16[128,1024]{1,0:T(8,128)(2,1)}), bf16[512,1024]{1,0:T(8,128)(2,1)}) %all-gather.8.cloned.1.call-update) | async-done | bytes 1048592 | tf_op jit(solution)/shard_map/all_gather | solution.py:89
  266.5 2.4 collective-permute-start.6
  269.9 2.4 broadcast_select_fusion.6
  272.4 2.4 pad_maximum_fusion.3
  274.8 3.9 copy.10
  278.7 3.9 copy.11
  282.6 2.8 bitcast_select_fusion
  285.5 6.2 %fusion.11 = f32[1024,896]{0,1:T(8,128)} fusion(bf16[1024,1024]{1,0:T(8,128)(2,1)S(1)} %bitcast_select_fusion, bf16[1024,1792]{1,0:T(8,128)(2,1)} %collective-permute-done.1), kind=kOutput, calls=%fused_computation.27 | convolution fusion | flops 1879048192 | bytes 7602176 | tf_op jit(solution)/shard_map/dot_general | solution.py:103
  291.8 5.7 %fusion.17 = f32[1024,896]{0,1:T(8,128)} fusion(bf16[1024,1024]{1,0:T(8,128)(2,1)S(1)} %bitcast_select_fusion, bf16[1024,1792]{1,0:T(8,128)(2,1)} %collective-permute-done.1), kind=kOutput, calls=%fused_computation.33 | convolution fusion | flops 1879048192 | bytes 7602176 | tf_op jit(solution)/shard_map/dot_general | solution.py:103
  298.4 6.3 %fusion.13 = f32[1024,896]{0,1:T(8,128)} fusion(bf16[1024,1024]{1,0:T(8,128)(2,1)S(1)} %bitcast_select_fusion.1, bf16[1024,1792]{1,0:T(8,128)(2,1)} %collective-permute-done), kind=kOutput, calls=%fused_computation.29 | convolution fusion | flops 1879048192 | bytes 7602176 | tf_op jit(solution)/shard_map/dot_general | solution.py:103
  304.7 5.5 %fusion.19 = f32[1024,896]{0,1:T(8,128)} fusion(bf16[1024,1024]{1,0:T(8,128)(2,1)S(1)} %bitcast_select_fusion.1, bf16[1024,1792]{1,0:T(8,128)(2,1)} %collective-permute-done), kind=kOutput, calls=%fused_computation.35 | convolution fusion | flops 1879048192 | bytes 7602176 | tf_op jit(solution)/shard_map/dot_general | solution.py:103
  310.2 1.4 broadcast_select_fusion.2
  311.6 1.6 fusion.68
  313.1 15.0 %copy.12 = bf16[1024,1024]{1,0:T(8,128)(2,1)} copy(bf16[1024,1024]{0,1:T(8,128)(2,1)} %fusion.68) | data formatting | bytes 4194304 | tf_op jit(solution)/shard_map/transpose | solution.py:97
  328.2 2.8 broadcast_select_fusion
  331.0 8.3 %fusion.76 = (bf16[1024,896]{0,1:T(8,128)(2,1)}, f32[1024,896]{0,1:T(8,128)S(1)}) fusion(bf16[1024,1024]{1,0:T(8,128)(2,1)S(1)} %broadcast_select_fusion, bf16[1024,1792]{1,0:T(8,128)(2,1)} %constant_dynamic-update-slice_fusion, f32[1024,896]{0,1:T(8,128)} %fusion.17, f32[1024,896]{0,1:T(8,128)} %fusion.19, f32[1024,896]{0,1:T(8,128)} %fusion.41, ...), kind=kOutput, calls=%fused_computation.81 | convolution fusion | flops 1887305728 | bytes 24121344 | tf_op jit(solution)/shard_map/dot_general | solution.py:103
  340.4 6.1 %fusion.75 = (bf16[1024,896]{0,1:T(8,128)(2,1)}, f32[1024,896]{0,1:T(8,128)S(1)}) fusion(bf16[1024,1024]{1,0:T(8,128)(2,1)S(1)} %broadcast_select_fusion, bf16[1024,1792]{1,0:T(8,128)(2,1)} %constant_dynamic-update-slice_fusion, f32[1024,896]{0,1:T(8,128)S(1)} %copy-done.4, f32[1024,896]{0,1:T(8,128)} %fusion.13, f32[1024,896]{0,1:T(8,128)S(1)} %copy-done.3, ...), kind=kOutput, calls=%fused_computation.80 | convolution fusion | flops 1887305728 | bytes 24121344 | tf_op jit(solution)/shard_map/dot_general | solution.py:103
  346.5 1.6 collective-permute-start.12
  348.2 1.5 collective-permute-start.11
  349.6 5.9 %fusion.71 = f32[1024,896]{0,1:T(8,128)} fusion(bf16[1024,896]{0,1:T(8,128)(2,1)} %get-tuple-element.25, bf16[512,1024]{0,1:T(8,128)(2,1)} %copy-done.15, bf16[512,512]{0,1:T(8,128)(2,1)} %bitcast.31, bf16[512,512]{0,1:T(8,128)(2,1)} %get-tuple-element.21), kind=kOutput, calls=%fused_computation.76 | convolution fusion | flops 1885339648 | bytes 7602176 | tf_op jit(solution)/shard_map/dot_general | solution.py:103
  355.6 2.1 fusion.72
  357.6 24.9 %collective-permute-done.8 = bf16[1024,896]{0,1:T(8,128)(2,1)} collective-permute-done((bf16[1024,896]{0,1:T(8,128)(2,1)}, bf16[1024,896]{0,1:T(8,128)(2,1)}, u32[]{:S(2)}, u32[]{:S(2)}) %collective-permute-start.8) | collective-permute-done | bytes 1835040 | tf_op jit(solution)/shard_map/ppermute | solution.py:20
  384.4 1.2 slice.125
  385.9 35.9 %collective-permute-done.12 = bf16[1024,896]{0,1:T(8,128)(2,1)S(1)} collective-permute-done((bf16[1024,896]{0,1:T(8,128)(2,1)}, bf16[1024,896]{0,1:T(8,128)(2,1)S(1)}, u32[]{:S(2)}, u32[]{:S(2)}) %collective-permute-start.12) | collective-permute-done | bytes 1835040 | tf_op jit(solution)/shard_map/ppermute | solution.py:20
  422.6 1.4 collective-permute-start.13
  424.0 5.5 %fusion.78 = f32[1024,896]{0,1:T(8,128)} fusion(bf16[1024,1024]{1,0:T(8,128)(2,1)S(1)} %copy-done.9, bf16[1024,896]{0,1:T(8,128)(2,1)} %collective-permute-done.8), kind=kOutput, calls=%fused_computation.83 | convolution fusion | flops 1879048192 | bytes 7602176 | tf_op jit(solution)/shard_map/dot_general | solution.py:103
  429.5 5.5 %fusion.77 = f32[1024,896]{0,1:T(8,128)} fusion(bf16[1024,1024]{1,0:T(8,128)(2,1)S(1)} %copy-done.11, bf16[1024,896]{0,1:T(8,128)(2,1)} %collective-permute-done.7), kind=kOutput, calls=%fused_computation.82 | convolution fusion | flops 1879048192 | bytes 7602176 | tf_op jit(solution)/shard_map/dot_general | solution.py:103
  435.1 3.9 fusion.80
  439.0 3.9 fusion.79
  444.8 8.0 %multiply_convert_fusion.1 = bf16[1024,896]{0,1:T(8,128)(2,1)S(1)} fusion(f32[1024,896]{0,1:T(8,128)} %fusion.78, f32[1024,896]{0,1:T(8,128)} %fusion.77, f32[1024,896]{0,1:T(8,128)} %fusion.71, f32[1024,896]{0,1:T(8,128)S(1)} %get-tuple-element.26, f32[1024,1792]{0,1:T(8,128)S(1)} %bitcast.29, bf16[1024,1024]{1,0:T(8,128)(2,1)S(1)} %broadcast_select_fusion, ...), kind=kOutput, calls=%fused_computation.6 | convolution fusion | flops 1890975744 | bytes 24121344 | tf_op jit(solution)/shard_map/dot_general | solution.py:103
  452.8 6.8 %collective-permute-done.14 = bf16[512,896]{0,1:T(8,128)(2,1)} collective-permute-done((bf16[512,896]{0,1:T(8,128)(2,1)S(1)}, bf16[512,896]{0,1:T(8,128)(2,1)}, u32[]{:S(2)}, u32[]{:S(2)}) %collective-permute-start.14) | collective-permute-done | bytes 917536 | tf_op jit(solution)/shard_map/ppermute | solution.py:20
  459.6 6.8 %multiply_convert_fusion = bf16[1024,896]{0,1:T(8,128)(2,1)S(1)} fusion(f32[1024,896]{0,1:T(8,128)} %fusion.80, f32[1024,896]{0,1:T(8,128)} %fusion.79, f32[1024,896]{0,1:T(8,128)S(1)} %fusion.72, f32[1024,896]{0,1:T(8,128)S(1)} %get-tuple-element.24, f32[1024,1792]{0,1:T(8,128)S(1)} %bitcast.29, bf16[1024,1024]{1,0:T(8,128)(2,1)S(1)} %broadcast_select_fusion, ...), kind=kOutput, calls=%fused_computation.4 | convolution fusion | flops 1890975744 | bytes 24121344 | tf_op jit(solution)/shard_map/dot_general | solution.py:103
  466.5 2.2 pad_maximum_fusion
  468.6 5.9 %copy.13 = bf16[1024,1792]{1,0:T(8,128)(2,1)} copy(bf16[1024,1792]{0,1:T(8,128)(2,1)} %pad_maximum_fusion) | data formatting | bytes 7340032 | tf_op jit(solution)/shard_map/concatenate | solution.py:116
  (89 shorter events, 11.6 us)
Async XLA Ops:
  6.5 47.2 %reduce-scatter.10.cloned.1.call-start = ((), (), s32[]{:S(2)}) async-start(), calls=%async_computation.8 | async-start | bytes 1966080
  15.5 82.7 %all-gather.4.cloned.1.call-start = ((), (), s32[]{:S(2)}) async-start(), calls=%async_computation.3 | async-start | bytes 1966080 | tf_op jit(solution)/shard_map/all_gather | solution.py:46
  15.6 82.7 %collective-permute-start.1 = (bf16[1024,1792]{1,0:T(8,128)(2,1)}, bf16[1024,1792]{1,0:T(8,128)(2,1)}, u32[]{:S(2)}, u32[]{:S(2)}) collective-permute-start(bf16[1024,1792]{1,0:T(8,128)(2,1)} %param.1), channel_id=1, source_target_pairs={{0,8},{4,12},{8,0},{12,4},{1,9},{5,13},{9,1},{13,5},{2,10},{6,14},... | collective-permute-start | bytes 11010056 | tf_op jit(solution)/shard_map/ppermute | solution.py:20
  18.6 81.1 %collective-permute-start = (bf16[1024,1792]{1,0:T(8,128)(2,1)}, bf16[1024,1792]{1,0:T(8,128)(2,1)}, u32[]{:S(2)}, u32[]{:S(2)}) collective-permute-start(bf16[1024,1792]{1,0:T(8,128)(2,1)} %param.1), channel_id=1, source_target_pairs={{0,4},{4,0},{8,12},{12,8},{1,5},{5,1},{9,13},{13,9},{2,6},{6,2},{1... | collective-permute-start | bytes 11010056 | tf_op jit(solution)/shard_map/ppermute | solution.py:20
  55.6 101.2 %reduce-scatter.6.cloned.1.call-start = ((), (), s32[]{:S(2)}) async-start(), calls=%async_computation.4 | async-start | bytes 2621440 | tf_op jit(solution)/shard_map/reduce_scatter | solution.py:86
  98.3 6.7 %copy-start.5 = (bf16[1024,1792]{1,0:T(8,128)(2,1)S(1)}, bf16[1024,1792]{1,0:T(8,128)(2,1)}, u32[]{:S(2)}) copy-start(bf16[1024,1792]{1,0:T(8,128)(2,1)} %param.1) | copy-start | bytes 11010052
  110.2 81.7 %reduce-scatter.8.cloned.1.call-start = ((), (), s32[]{:S(2)}) async-start(), calls=%async_computation.6 | async-start | bytes 1310720 | tf_op jit(solution)/shard_map/reduce_scatter | solution.py:86
  111.8 40.9 %collective-permute-start.4 = (bf16[512,1792]{1,0:T(8,128)(2,1)S(1)}, bf16[512,1792]{1,0:T(8,128)(2,1)S(1)}, u32[]{:S(2)}, u32[]{:S(2)}) collective-permute-start(bf16[512,1792]{1,0:T(8,128)(2,1)S(1)} %slice.122), channel_id=1, source_target_pairs={{0,8},{4,12},{8,0},{12,4},{1,9},{5,13},{9,1},{13,5},{2,10},{6,14},... | collective-permute-start | bytes 5505032 | tf_op jit(solution)/shard_map/ppermute | solution.py:20
  114.0 41.5 %collective-permute-start.5 = (bf16[512,1792]{1,0:T(8,128)(2,1)S(1)}, bf16[512,1792]{1,0:T(8,128)(2,1)S(1)}, u32[]{:S(2)}, u32[]{:S(2)}) collective-permute-start(bf16[512,1792]{1,0:T(8,128)(2,1)S(1)} %slice.123), channel_id=1, source_target_pairs={{0,4},{4,0},{8,12},{12,8},{1,5},{5,1},{9,13},{13,9},{2,6},{6,2},{1... | collective-permute-start | bytes 5505032 | tf_op jit(solution)/shard_map/ppermute | solution.py:20
  163.1 75.1 %all-gather.6.cloned.1.call-start = ((), (), s32[]{:S(2)}) async-start(), calls=%async_computation.5 | async-start | bytes 2621440 | tf_op jit(solution)/shard_map/all_gather | solution.py:89
  163.7 102.9 %all-gather.8.cloned.1.call-start = ((), (), s32[]{:S(2)}) async-start(), calls=%async_computation.7 | async-start | bytes 1310720 | tf_op jit(solution)/shard_map/all_gather | solution.py:89
  191.8 3.1 copy-start
  198.8 45.4 %copy-start.7 = (bf16[512,1536]{0,1:T(8,128)(2,1)S(1)}, bf16[512,1536]{0,1:T(8,128)(2,1)}, u32[]{:S(2)}) copy-start(bf16[512,1536]{0,1:T(8,128)(2,1)} %all-gather.4.cloned.1.call-done) | copy-start | bytes 4718596
  241.2 27.7 %collective-permute-start.2 = (bf16[512,1024]{1,0:T(8,128)(2,1)}, bf16[512,1024]{1,0:T(8,128)(2,1)S(1)}, u32[]{:S(2)}, u32[]{:S(2)}) collective-permute-start(bf16[512,1024]{1,0:T(8,128)(2,1)} %get-tuple-element.19), channel_id=1, source_target_pairs={{0,4},{4,0},{8,12},{12,8},{1,5},{5,1},{9,13},{13,9},{2,6},{6,2},{1... | collective-permute-start | bytes 3145736 | tf_op jit(solution)/shard_map/ppermute | solution.py:20
  242.7 27.2 %collective-permute-start.3 = (bf16[512,1024]{1,0:T(8,128)(2,1)}, bf16[512,1024]{1,0:T(8,128)(2,1)}, u32[]{:S(2)}, u32[]{:S(2)}) collective-permute-start(bf16[512,1024]{1,0:T(8,128)(2,1)} %get-tuple-element.20), channel_id=1, source_target_pairs={{0,8},{4,12},{8,0},{12,4},{1,9},{5,13},{9,1},{13,5},{2,10},{6,14},... | collective-permute-start | bytes 3145736 | tf_op jit(solution)/shard_map/ppermute | solution.py:20
  246.1 6.2 %copy-start.15 = (bf16[512,1024]{0,1:T(8,128)(2,1)}, bf16[512,1024]{0,1:T(8,128)(2,1)S(1)}, u32[]{:S(2)}) copy-start(bf16[512,1024]{0,1:T(8,128)(2,1)S(1)} %slice.117) | copy-start | bytes 3145732
  246.1 6.2 %copy-start.6 = (bf16[1024,1792]{1,0:T(8,128)(2,1)S(1)}, bf16[1024,1792]{1,0:T(8,128)(2,1)}, u32[]{:S(2)}) copy-start(bf16[1024,1792]{1,0:T(8,128)(2,1)} %param.1) | copy-start | bytes 11010052
  246.1 6.2 %copy-start.19 = (bf16[512,512]{1,0:T(8,128)(2,1)S(1)}, bf16[512,512]{1,0:T(8,128)(2,1)}, u32[]{:S(2)}) copy-start(bf16[512,512]{1,0:T(8,128)(2,1)} %copy.16) | copy-start | bytes 1572868
  246.1 6.2 %copy-start.21 = (bf16[512,512]{0,1:T(8,128)(2,1)S(1)}, bf16[512,512]{0,1:T(8,128)(2,1)}, u32[]{:S(2)}) copy-start(bf16[512,512]{0,1:T(8,128)(2,1)} %get-tuple-element.21) | copy-start | bytes 1572868
  266.5 43.7 %collective-permute-start.6 = (bf16[512,1024]{1,0:T(8,128)(2,1)}, bf16[512,1024]{1,0:T(8,128)(2,1)}, u32[]{:S(2)}, u32[]{:S(2)}) collective-permute-start(bf16[512,1024]{1,0:T(8,128)(2,1)} %all-gather.8.cloned.1.call-done), channel_id=1, source_target_pairs={{0,12},{4,8},{8,4},{12,0},{1,13},{5,9},{9,5},{13,1},{2,14},{6,10},... | collective-permute-start | bytes 3145736 | tf_op jit(solution)/shard_map/ppermute | solution.py:20
  268.9 1.0 copy-start.14
  272.3 2.4 copy-start.1
  285.5 6.3 %copy-start.8 = (bf16[1024,1024]{1,0:T(8,128)(2,1)}, bf16[1024,1024]{1,0:T(8,128)(2,1)S(1)}, u32[]{:S(2)}) copy-start(bf16[1024,1024]{1,0:T(8,128)(2,1)S(1)} %bitcast_select_fusion) | copy-start | bytes 6291460
  291.8 5.7 %copy-start.2 = (bf16[1024,1024]{0,1:T(8,128)(2,1)S(1)}, bf16[1024,1024]{0,1:T(8,128)(2,1)}, u32[]{:S(2)}) copy-start(bf16[1024,1024]{0,1:T(8,128)(2,1)} %copy.10) | copy-start | bytes 6291460
  298.4 6.3 %copy-start.10 = (bf16[1024,1024]{1,0:T(8,128)(2,1)}, bf16[1024,1024]{1,0:T(8,128)(2,1)S(1)}, u32[]{:S(2)}) copy-start(bf16[1024,1024]{1,0:T(8,128)(2,1)S(1)} %bitcast_select_fusion.1) | copy-start | bytes 6291460
  304.7 5.5 %copy-start.13 = (bf16[512,1024]{1,0:T(8,128)(2,1)S(1)}, bf16[512,1024]{1,0:T(8,128)(2,1)}, u32[]{:S(2)}) copy-start(bf16[512,1024]{1,0:T(8,128)(2,1)} %all-gather.8.cloned.1.call-done) | copy-start | bytes 3145732
  328.2 11.7 %slice-start = ((s8[7340032]{0:T(1024)(128)(4,1)}), s8[4194304]{0:T(1024)(128)(4,1)S(1)}, s32[]{:S(2)}) async-start(s8[7340032]{0:T(1024)(128)(4,1)} %bitcast.28), calls=%async_computation.9 | async-start | bytes 8388608
  331.0 8.9 %slice-start.1 = ((s8[7340032]{0:T(1024)(128)(4,1)}), s8[3145728]{0:T(1024)(128)(4,1)S(1)}, s32[]{:S(2)}) async-start(s8[7340032]{0:T(1024)(128)(4,1)} %bitcast.28), calls=%async_computation.10 | async-start | bytes 6291456
  331.0 8.9 %copy-start.3 = (f32[1024,896]{0,1:T(8,128)S(1)}, f32[1024,896]{0,1:T(8,128)}, u32[]{:S(2)}) copy-start(f32[1024,896]{0,1:T(8,128)} %fusion.33) | copy-start | bytes 11010052
  331.0 9.4 %copy-start.4 = (f32[1024,896]{0,1:T(8,128)S(1)}, f32[1024,896]{0,1:T(8,128)}, u32[]{:S(2)}) copy-start(f32[1024,896]{0,1:T(8,128)} %fusion.11) | copy-start | bytes 11010052
  339.3 43.3 %collective-permute-start.8 = (bf16[1024,896]{0,1:T(8,128)(2,1)}, bf16[1024,896]{0,1:T(8,128)(2,1)}, u32[]{:S(2)}, u32[]{:S(2)}) collective-permute-start(bf16[1024,896]{0,1:T(8,128)(2,1)} %get-tuple-element.25), channel_id=1, source_target_pairs={{0,8},{4,12},{8,0},{12,4},{1,9},{5,13},{9,1},{13,5},{2,10},{6,14},... | collective-permute-start | bytes 5505032 | tf_op jit(solution)/shard_map/ppermute | solution.py:20
  339.3 45.1 %collective-permute-start.7 = (bf16[1024,896]{0,1:T(8,128)(2,1)}, bf16[1024,896]{0,1:T(8,128)(2,1)}, u32[]{:S(2)}, u32[]{:S(2)}) collective-permute-start(bf16[1024,896]{0,1:T(8,128)(2,1)} %get-tuple-element.25), channel_id=1, source_target_pairs={{0,4},{4,0},{8,12},{12,8},{1,5},{5,1},{9,13},{13,9},{2,6},{6,2},{1... | collective-permute-start | bytes 5505032 | tf_op jit(solution)/shard_map/ppermute | solution.py:20
  346.5 9.0 %copy-start.12 = (bf16[1024,896]{0,1:T(8,128)(2,1)S(1)}, bf16[1024,896]{0,1:T(8,128)(2,1)}, u32[]{:S(2)}) copy-start(bf16[1024,896]{0,1:T(8,128)(2,1)} %get-tuple-element.23) | copy-start | bytes 5505028
  346.5 9.0 %copy-start.16 = (bf16[512,1024]{0,1:T(8,128)(2,1)S(1)}, bf16[512,1024]{0,1:T(8,128)(2,1)}, u32[]{:S(2)}) copy-start(bf16[512,1024]{0,1:T(8,128)(2,1)} %copy-done.15) | copy-start | bytes 3145732
  346.5 9.0 %copy-start.20 = (bf16[512,512]{1,0:T(8,128)(2,1)S(1)}, bf16[512,512]{1,0:T(8,128)(2,1)}, u32[]{:S(2)}) copy-start(bf16[512,512]{1,0:T(8,128)(2,1)} %copy.16) | copy-start | bytes 1572868
  346.5 9.0 %copy-start.22 = (bf16[512,512]{0,1:T(8,128)(2,1)S(1)}, bf16[512,512]{0,1:T(8,128)(2,1)}, u32[]{:S(2)}) copy-start(bf16[512,512]{0,1:T(8,128)(2,1)} %get-tuple-element.21) | copy-start | bytes 1572868
  346.5 75.2 %collective-permute-start.12 = (bf16[1024,896]{0,1:T(8,128)(2,1)}, bf16[1024,896]{0,1:T(8,128)(2,1)S(1)}, u32[]{:S(2)}, u32[]{:S(2)}) collective-permute-start(bf16[1024,896]{0,1:T(8,128)(2,1)} %get-tuple-element.23), channel_id=1, source_target_pairs={{0,8},{4,12},{8,0},{12,4},{1,9},{5,13},{9,1},{13,5},{2,10},{6,14},... | collective-permute-start | bytes 5505032 | tf_op jit(solution)/shard_map/ppermute | solution.py:20
  348.2 74.4 %collective-permute-start.11 = (bf16[1024,896]{0,1:T(8,128)(2,1)}, bf16[1024,896]{0,1:T(8,128)(2,1)S(1)}, u32[]{:S(2)}, u32[]{:S(2)}) collective-permute-start(bf16[1024,896]{0,1:T(8,128)(2,1)} %get-tuple-element.23), channel_id=1, source_target_pairs={{0,4},{4,0},{8,12},{12,8},{1,5},{5,1},{9,13},{13,9},{2,6},{6,2},{1... | collective-permute-start | bytes 5505032 | tf_op jit(solution)/shard_map/ppermute | solution.py:20
  357.6 66.4 %copy-start.9 = (bf16[1024,1024]{1,0:T(8,128)(2,1)S(1)}, bf16[1024,1024]{1,0:T(8,128)(2,1)}, u32[]{:S(2)}) copy-start(bf16[1024,1024]{1,0:T(8,128)(2,1)} %copy-done.8) | copy-start | bytes 6291460
  383.8 59.1 %collective-permute-start.10 = (bf16[512,896]{0,1:T(8,128)(2,1)S(1)}, bf16[512,896]{0,1:T(8,128)(2,1)S(1)}, u32[]{:S(2)}, u32[]{:S(2)}) collective-permute-start(bf16[512,896]{0,1:T(8,128)(2,1)S(1)} %slice.126), channel_id=1, source_target_pairs={{0,4},{4,0},{8,12},{12,8},{1,5},{5,1},{9,13},{13,9},{2,6},{6,2},{1... | collective-permute-start | bytes 2752520 | tf_op jit(solution)/shard_map/ppermute | solution.py:20
  385.7 57.2 %collective-permute-start.9 = (bf16[512,896]{0,1:T(8,128)(2,1)S(1)}, bf16[512,896]{0,1:T(8,128)(2,1)S(1)}, u32[]{:S(2)}, u32[]{:S(2)}) collective-permute-start(bf16[512,896]{0,1:T(8,128)(2,1)S(1)} %slice.125), channel_id=1, source_target_pairs={{0,8},{4,12},{8,0},{12,4},{1,9},{5,13},{9,1},{13,5},{2,10},{6,14},... | collective-permute-start | bytes 2752520 | tf_op jit(solution)/shard_map/ppermute | solution.py:20
  421.9 37.7 %collective-permute-start.14 = (bf16[512,896]{0,1:T(8,128)(2,1)S(1)}, bf16[512,896]{0,1:T(8,128)(2,1)}, u32[]{:S(2)}, u32[]{:S(2)}) collective-permute-start(bf16[512,896]{0,1:T(8,128)(2,1)S(1)} %slice.132), channel_id=1, source_target_pairs={{0,4},{4,0},{8,12},{12,8},{1,5},{5,1},{9,13},{13,9},{2,6},{6,2},{1... | collective-permute-start | bytes 2752520 | tf_op jit(solution)/shard_map/ppermute | solution.py:20
  422.6 6.9 %copy-start.11 = (bf16[1024,1024]{1,0:T(8,128)(2,1)S(1)}, bf16[1024,1024]{1,0:T(8,128)(2,1)}, u32[]{:S(2)}) copy-start(bf16[1024,1024]{1,0:T(8,128)(2,1)} %copy-done.10) | copy-start | bytes 6291460
  422.6 37.0 %collective-permute-start.13 = (bf16[512,896]{0,1:T(8,128)(2,1)S(1)}, bf16[512,896]{0,1:T(8,128)(2,1)}, u32[]{:S(2)}, u32[]{:S(2)}) collective-permute-start(bf16[512,896]{0,1:T(8,128)(2,1)S(1)} %slice.131), channel_id=1, source_target_pairs={{0,8},{4,12},{8,0},{12,4},{1,9},{5,13},{9,1},{13,5},{2,10},{6,14},... | collective-permute-start | bytes 2752520 | tf_op jit(solution)/shard_map/ppermute | solution.py:20
  442.9 0.9 copy-start.17
  443.9 0.9 copy-start.18
Sparse Core Ops, SparseCore 0:
  15.7 37.9 reduce-scatter.9
  55.8 36.6 all-gather.3
  110.3 45.3 reduce-scatter.5
  163.2 28.5 reduce-scatter.7
  193.2 44.8 all-gather.5
  239.6 26.9 all-gather.7
